TPU v7x, 128 devices: a whole 4x4x4 slice. The times are simulated.
128 devices in a mesh: blk: 4 (over z_lo, core), grp: 32 (over x, y, z_hi).
Axes of the slice: x: 4, y: 4, z: 4 (z_hi: 2, z_lo: 2; z = z_hi * 2 + z_lo), core: 2. Of those that a mesh axis runs over, the one named last changes fastest.
Arguments:
- features: bfloat16 [131072, 1024], P(('blk', 'grp')), may hold values from -24 to 24
- tiles: bfloat16 [1024, 24, 128, 128], P(('blk', 'grp')), may hold values from 0 to 1, as said below
- slots: int32 [1024, 24], P(('blk', 'grp')), may hold values from 0 to 1023, as said below
- w_self: bfloat16 [1024, 1024], replicated, may hold values from -0.1875 to 0.1875
- w_neigh: bfloat16 [1024, 1024], replicated, may hold values from -0.375 to 0.375
- cotangent: bfloat16 [131072, 1024], P(('blk', 'grp')), may hold values from -0.016479492 to 0.016479492
Outputs:
- hidden: bfloat16 [131072, 1024], P(('blk', 'grp'))
- grad_self: float32 [1024, 1024], P(('blk', 'grp'))
- grad_neigh: float32 [1024, 1024], P(('blk', 'grp'))
Inputs may be any that keep to these rules, and one draw needn't show every extreme that they name: Nodes are laid out device by device: device d = b * 32 + g (b the index of blk, g of grp) holds row blocks d * 8 onward. Each row block has a live count c of 1 to 24; slots 0 to c-1 name distinct column blocks, each held by the row block's own device or by device (b, g-1), (b, g+1), (b-1, g) or (b+1, g), indices taken modulo 32 and 4; slots c and after repeat slot 0. The first row block of every device has c = 24, and its live slots name column blocks of all five of those devices. Tiles of slots at or after a row block's live count are zero; live tiles have every entry positive, at least 0.05.
All inputs are finite; a program needn't handle non-finite values.
Results may differ from a plain program's by a relative error of at most 0.0049.
Values may be sent and summed in bfloat16 or wider, within the bound.
A program may use at most 128 MiB of HBM per device.

v0:
```python
import jax
import jax.numpy as jnp
from jax import lax
from jax.sharding import PartitionSpec as P

BLOCK = 128


def passed_along(array, axis, by):
    peers = lax.axis_size(axis)
    return lax.ppermute(array, axis, [(i, (i + by) % peers) for i in range(peers)])


def gelu_tanh(v):
    return jax.nn.gelu(v, approximate=True)


def on_device(features, tiles, slots, w_self, w_neigh, cotangent):
    group_count = lax.axis_size("blk")
    member_count = lax.axis_size("grp")
    my_group = lax.axis_index("blk")
    my_member = lax.axis_index("grp")
    prev_member = passed_along(features, "grp", 1)
    next_member = passed_along(features, "grp", -1)
    prev_group = passed_along(features, "blk", 1)
    next_group = passed_along(features, "blk", -1)
    width = features.shape[1]
    local_blocks = tiles.shape[0]
    sources = jnp.stack((features, prev_member, next_member, prev_group, next_group))
    sources = sources.reshape(5, local_blocks, BLOCK, width)
    owner = slots // local_blocks
    inner = slots % local_blocks
    owner_group = owner // member_count
    owner_member = owner % member_count
    same_group = owner_group == my_group
    source_id = jnp.where(
        same_group & (owner_member == my_member),
        0,
        jnp.where(
            same_group & (owner_member == (my_member - 1) % member_count),
            1,
            jnp.where(same_group, 2, jnp.where(owner_group == (my_group - 1) % group_count, 3, 4)),
        ),
    ).astype(jnp.int32)

    def add_slot(slot, total):
        chosen = sources[source_id[:, slot], inner[:, slot]]
        return total + jnp.einsum(
            "rab,rbf->raf", tiles[:, slot], chosen, preferred_element_type=jnp.float32
        )

    start = jnp.zeros((local_blocks, BLOCK, width), jnp.float32)
    total = lax.fori_loop(0, tiles.shape[1], add_slot, start)
    degree = jnp.sum(tiles.astype(jnp.float32), axis=(1, 3))
    mean_neigh = (total / degree[:, :, None]).astype(jnp.bfloat16).reshape(features.shape[0], width)
    pre = jnp.dot(features, w_self, preferred_element_type=jnp.float32)
    pre = pre + jnp.dot(mean_neigh, w_neigh, preferred_element_type=jnp.float32)
    hidden = gelu_tanh(pre).astype(jnp.bfloat16)
    slope = jax.vjp(gelu_tanh, pre)[1]
    dpre = slope(cotangent.astype(jnp.float32))[0].astype(jnp.bfloat16)
    term_self = lax.dot_general(
        features, dpre, (((0,), (0,)), ((), ())), preferred_element_type=jnp.float32
    )
    term_neigh = lax.dot_general(
        mean_neigh, dpre, (((0,), (0,)), ((), ())), preferred_element_type=jnp.float32
    )
    grad_self, grad_neigh = (
        lax.psum_scatter(term_self, ("blk", "grp"), scatter_dimension=0, tiled=True),
        lax.psum_scatter(term_neigh, ("blk", "grp"), scatter_dimension=0, tiled=True),
    )
    return (hidden, grad_self, grad_neigh)


def solution(mesh):
    in_specs = (
        P(("blk", "grp"), None),
        P(("blk", "grp"), None, None, None),
        P(("blk", "grp"), None),
        P(),
        P(),
        P(("blk", "grp"), None),
    )
    out_specs = (P(("blk", "grp"), None), P(("blk", "grp"), None), P(("blk", "grp"), None))
    return jax.shard_map(
        on_device, mesh=mesh, in_specs=in_specs, out_specs=out_specs, check_vma=False
    )
```

profile of v0, /device:TPU:0, one launch (start us, length us, event | category | flops | bytes accessed | tf_op | source)
XLA Modules:
  0.0 1781.4 jit_solution(16643662530813344345)
XLA Ops:
  7.2 4.0 collective-permute-start
  11.3 4.7 collective-permute-start.1
  20.3 3.8 convert_reduce_fusion
  24.3 4.4 fusion.17
  28.7 73.9 %collective-permute-done = bf16[1024,1024]{1,0:T(8,128)(2,1)} collective-permute-done((bf16[1024,1024]{1,0:T(8,128)(2,1)}, bf16[1024,1024]{1,0:T(8,128)(2,1)}, u32[]{:S(2)}, u32[]{:S(2)}) %collective-permute-start) | collective-permute-done | bytes 2097184 | tf_op jit(solution)/shard_map/ppermute | solution.py:11
  104.3 2.3 collective-permute-done.1
  108.3 38.3 %collective-permute-done.2 = bf16[1024,1024]{1,0:T(8,128)(2,1)} collective-permute-done((bf16[1024,1024]{1,0:T(8,128)(2,1)}, bf16[1024,1024]{1,0:T(8,128)(2,1)}, u32[]{:S(2)}, u32[]{:S(2)}) %collective-permute-start.2) | collective-permute-done | bytes 2097184 | tf_op jit(solution)/shard_map/ppermute | solution.py:11
  150.2 4.0 copy-done.1
  154.2 276.5 %while.14 = (s32[]{:T(128)}, f32[8,128,1024]{2,1,0:T(8,128)}, bf16[8,24,128,128]{3,2,1,0:T(8,128)(2,1)}, s32[8,24]{0,1:T(8,128)S(1)}, s32[8,24]{0,1:T(8,128)S(1)...) while((s32[]{:T(128)}, f32[8,128,1024]{2,1,0:T(8,128)}, ...), condition=%wide.region_1.2_spmd.clone, body=%wide.region_0.1_spmd.clone.sunk | while | flops 270532704 | bytes 14942979 | solution.py:53
  154.2 6.0 gather_fusion
  160.2 4.4 select_add_fusion.2
  164.5 6.0 gather_fusion
  170.5 5.6 select_add_fusion.2
  176.1 6.0 gather_fusion
  182.1 5.6 select_add_fusion.2
  187.7 6.0 gather_fusion
  193.7 5.6 select_add_fusion.2
  199.3 6.0 gather_fusion
  205.2 5.6 select_add_fusion.2
  210.8 6.0 gather_fusion
  216.8 5.6 select_add_fusion.2
  222.4 6.0 gather_fusion
  228.4 5.6 select_add_fusion.2
  234.0 6.0 gather_fusion
  240.0 5.6 select_add_fusion.2
  245.6 6.0 gather_fusion
  251.5 5.6 select_add_fusion.2
  257.1 6.0 gather_fusion
  263.1 5.6 select_add_fusion.2
  268.7 6.0 gather_fusion
  274.7 5.6 select_add_fusion.2
  280.3 6.0 gather_fusion
  286.3 5.6 select_add_fusion.2
  291.9 6.0 gather_fusion
  297.8 5.6 select_add_fusion.2
  303.4 6.0 gather_fusion
  309.4 5.6 select_add_fusion.2
  315.0 6.0 gather_fusion
  321.0 5.6 select_add_fusion.2
  326.6 6.0 gather_fusion
  332.6 5.6 select_add_fusion.2
  338.2 6.0 gather_fusion
  344.1 5.6 select_add_fusion.2
  349.7 6.0 gather_fusion
  355.7 5.6 select_add_fusion.2
  361.3 6.0 gather_fusion
  367.3 5.6 select_add_fusion.2
  372.9 6.0 gather_fusion
  378.9 5.6 select_add_fusion.2
  384.5 6.0 gather_fusion
  390.4 5.6 select_add_fusion.2
  396.0 6.0 gather_fusion
  402.0 5.6 select_add_fusion.2
  407.6 6.0 gather_fusion
  413.6 5.6 select_add_fusion.2
  419.2 6.0 gather_fusion
  425.2 5.6 select_add_fusion.2
  430.7 2.9 divide_convert_fusion
  434.8 6.4 fusion.5
  442.6 4.4 fusion.18
  447.2 6.6 convolution_bitcast_fusion
  453.8 5.4 copy.21
  459.2 653.4 %reduce-scatter.5.cloned.1.call-done = f32[8,1024]{1,0:T(8,128)} async-done(((f32[1024,1024]{1,0:T(8,128)}), f32[8,1024]{1,0:T(8,128)}) %reduce-scatter.5.cloned.1.call-update) | async-done | bytes 32784 | tf_op jit(solution)/shard_map/reduce_scatter | solution.py:69
  1112.6 661.9 %reduce-scatter.7.cloned.1.call-done = f32[8,1024]{1,0:T(8,128)} async-done(((f32[1024,1024]{1,0:T(8,128)}), f32[8,1024]{1,0:T(8,128)}) %reduce-scatter.7.cloned.1.call-update) | async-done | bytes 32784
  (52 shorter events, 14.7 us)
Async XLA Ops:
  7.2 426.4 %copy-start = (bf16[1024,1024]{1,0:T(8,128)(2,1)S(1)}, bf16[1024,1024]{1,0:T(8,128)(2,1)}, u32[]{:S(2)}) copy-start(bf16[1024,1024]{1,0:T(8,128)(2,1)} %param.12) | copy-start | bytes 6291460
  7.2 1105.5 %reduce-scatter.5.cloned.1.call-start = ((), (), s32[]{:S(2)}) async-start(), calls=%async_computation.2 | async-start | bytes 4227072 | tf_op jit(solution)/shard_map/reduce_scatter | solution.py:69
  7.2 95.3 %collective-permute-start = (bf16[1024,1024]{1,0:T(8,128)(2,1)}, bf16[1024,1024]{1,0:T(8,128)(2,1)}, u32[]{:S(2)}, u32[]{:S(2)}) collective-permute-start(bf16[1024,1024]{1,0:T(8,128)(2,1)} %param.8), channel_id=1, source_target_pairs={{0,1},{1,2},{2,3},{3,4},{4,5},{5,6},{6,7},{7,8},{8,9},{9,10},{10,1... | collective-permute-start | bytes 6291464 | tf_op jit(solution)/shard_map/ppermute | solution.py:11
  11.3 95.3 %collective-permute-start.1 = (bf16[1024,1024]{1,0:T(8,128)(2,1)}, bf16[1024,1024]{1,0:T(8,128)(2,1)}, u32[]{:S(2)}, u32[]{:S(2)}) collective-permute-start(bf16[1024,1024]{1,0:T(8,128)(2,1)} %param.8), channel_id=1, source_target_pairs={{0,31},{1,0},{2,1},{3,2},{4,3},{5,4},{6,5},{7,6},{8,7},{9,8},{10,9... | collective-permute-start | bytes 6291464 | tf_op jit(solution)/shard_map/ppermute | solution.py:11
  16.0 130.7 %collective-permute-start.2 = (bf16[1024,1024]{1,0:T(8,128)(2,1)}, bf16[1024,1024]{1,0:T(8,128)(2,1)}, u32[]{:S(2)}, u32[]{:S(2)}) collective-permute-start(bf16[1024,1024]{1,0:T(8,128)(2,1)} %param.8), channel_id=1, source_target_pairs={{0,32},{32,64},{64,96},{96,0},{1,33},{33,65},{65,97},{97,1},{2,34}... | collective-permute-start | bytes 6291464 | tf_op jit(solution)/shard_map/ppermute | solution.py:11
  16.0 132.4 %collective-permute-start.3 = (bf16[1024,1024]{1,0:T(8,128)(2,1)}, bf16[1024,1024]{1,0:T(8,128)(2,1)}, u32[]{:S(2)}, u32[]{:S(2)}) collective-permute-start(bf16[1024,1024]{1,0:T(8,128)(2,1)} %param.8), channel_id=1, source_target_pairs={{0,96},{32,0},{64,32},{96,64},{1,97},{33,1},{65,33},{97,65},{2,98}... | collective-permute-start | bytes 6291464 | tf_op jit(solution)/shard_map/ppermute | solution.py:11
  20.3 3.9 copy-start.2
  20.3 4.0 copy-start.3
  150.2 4.0 copy-start.1
  430.7 2.9 copy-start.4
  430.7 4.1 copy-start.5
  441.2 1.4 copy-start.6
  447.0 1327.6 %reduce-scatter.7.cloned.1.call-start = ((), (), s32[]{:S(2)}) async-start(), calls=%async_computation.3 | async-start | bytes 4227072
Sparse Core Ops, SparseCore 0:
  447.1 665.4 reduce-scatter.4
  1115.7 658.8 reduce-scatter.6
where the time goes:
time: 1780 us
  waiting for transfers between devices  1430 us (80%)
  local copies, waits for them, and re-layouts  165 us (9%)
  matrix products  154 us (9%)
    unnamed x3, waiting for transfers between devices  662 us
    reduce_scatter x1, waiting for transfers between devices, on_device(): lax.psum_scatter(term_neigh, ('blk', 'grp'), scatter_dimension=0, tiled=T...  653 us
    gather x24, local copies, waits for them, and re-layouts, add_slot(): chosen = sources[source_id[:, slot], inner[:, slot]]  144 us
    dot_general x24, matrix products, add_slot(): jnp.einsum('rab,rbf->raf', tiles[:, slot], chosen, preferred_element_type...  133 us
    ppermute x4, waiting for transfers between devices, passed_along(): lax.ppermute(array, axis, [(i, (i + by) % peers) for i in range(peers)])  114 us
  transfers between devices with their start and end apart: 6, of which 5 were waited for; matrix products, arithmetic and copies ran while one was open for 2% of the time, Pallas kernels for 0%

commit v1 on v0

v1 whole, which is shorter than its diff:
```python
import functools

import jax
import jax.numpy as jnp
from jax import lax
from jax.experimental import pallas as pl
from jax.experimental.pallas import tpu as pltpu
from jax.sharding import PartitionSpec as P

MESH = pl.DeviceIdType.MESH
BLOCK = 128
SLOTS = 24
ROWS = 1024
DIM = 1024
COLS = 256
CHUNKS = DIM // COLS
BLOCKS = ROWS // BLOCK
N_GRP = 32
PIECES = CHUNKS * BLOCKS
AHEAD = 4
UNITS = 2 * CHUNKS
F32 = jnp.float32
BF16 = jnp.bfloat16


def loop(count, body):
    lax.fori_loop(0, count, lambda i, _: (body(i), None)[1], None)


def kernel(
    inv_ref, feat_ref, tiles_ref, ws_ref, wn_ref, cot_ref,
    hidden_ref, gs_ref, gn_ref,
    src, adj, tbuf_even, tbuf_odd, ws, wn, cot, pre, total, feat_t, mean_t, mean, rinv, dpre, hid,
    core_out, core_in, s1_out, s1_in, acc1, s2_out, s2_in, acc2, s3_in,
    local_sem, tile_sem, hid_sem, fc_sem, fc_recv, f_send, f1_recv, f2_recv, f3_recv,
    core_send, core_recv, s1_send, s1_recv, s2_send, s2_recv, s3_send, s3_recv,
):
    b = lax.axis_index("blk")
    g = lax.axis_index("grp")
    z_lo = b // 2
    core = b % 2
    z_hi = g % 2
    y = (g // 2) % 4
    x = g // 8

    def at(bb, gg):
        return (bb, gg)

    core_peer = at(z_lo * 2 + (1 - core), g)
    z_peer = at(3 - b, g)
    hi_peer = at(3 - b, z_hi * (g - 1) + (1 - z_hi) * (g + 1))
    step = 2 - 4 * z_hi
    out_peer = at(b, (g + step + N_GRP) % N_GRP)
    in_peer = at(b, (g - step + N_GRP) % N_GRP)

    def x_peer(d):
        return at(b, ((x + d) % 4) * 8 + y * 2 + z_hi)

    def y_peer(d):
        return at(b, x * 8 + ((y + d) % 4) * 2 + z_hi)

    def z_ring(d):
        lo = (z_lo + d % 2) % 2
        hi = (z_hi + d // 2) % 2
        return lo, hi

    def z_dev(d):
        lo, hi = z_ring(d)
        return at(lo * 2 + core, x * 8 + y * 2 + hi)

    peers = [core_peer, z_peer, hi_peer, out_peer, in_peer]
    for d in (1, 2, 3):
        peers += [x_peer(d), y_peer(d), z_dev(d)]

    def feat_copy(c):
        return pltpu.make_async_copy(
            feat_ref.at[:, pl.ds(c * COLS, COLS)], src.at[0, c], local_sem.at[c])

    tile_bufs = (tbuf_even, tbuf_odd)

    def tile_copy(r, slot):
        return pltpu.make_async_copy(
            tiles_ref.at[r], tile_bufs[slot].at[pl.ds(0, SLOTS)], tile_sem.at[slot])

    ws_copy = pltpu.make_async_copy(ws_ref, ws, local_sem.at[4])
    wn_copy = pltpu.make_async_copy(wn_ref, wn, local_sem.at[5])
    cot_copy = pltpu.make_async_copy(cot_ref, cot, local_sem.at[6])

    barrier = pltpu.get_barrier_semaphore()
    for p in peers:
        pl.semaphore_signal(barrier, inc=1, device_id=p, device_id_type=MESH)
    tile_copy(0, 0).start()
    for c in range(CHUNKS):
        feat_copy(c).start()
    ws_copy.start()
    pl.semaphore_wait(barrier, len(peers))

    def piece(p):
        return p // BLOCKS, pl.ds(pl.multiple_of((p % BLOCKS) * BLOCK, BLOCK), BLOCK)

    def f1(p):
        c, rows = piece(p)
        return pltpu.make_async_remote_copy(
            src_ref=feat_ref.at[rows, pl.ds(pl.multiple_of(c * COLS, COLS), COLS)],
            dst_ref=src.at[2, c, rows],
            send_sem=f_send.at[0], recv_sem=f1_recv.at[p],
            device_id=z_peer, device_id_type=MESH)

    def f2(p):
        c, rows = piece(p)
        return pltpu.make_async_remote_copy(
            src_ref=src.at[2, c, rows], dst_ref=src.at[3, c, rows],
            send_sem=f_send.at[1], recv_sem=f2_recv.at[p],
            device_id=hi_peer, device_id_type=MESH)

    def f3(p):
        c, rows = piece(p)
        return pltpu.make_async_remote_copy(
            src_ref=src.at[3, c, rows], dst_ref=src.at[4, c, rows],
            send_sem=f_send.at[2], recv_sem=f3_recv.at[p],
            device_id=out_peer, device_id_type=MESH)

    def fc(c):
        return pltpu.make_async_remote_copy(
            src_ref=feat_ref.at[:, pl.ds(pl.multiple_of(c * COLS, COLS), COLS)],
            dst_ref=src.at[1, c],
            send_sem=fc_sem.at[c], recv_sem=fc_recv.at[c],
            device_id=core_peer, device_id_type=MESH)

    for p in range(AHEAD):
        f1(p).start()
    for c in range(CHUNKS):
        fc(c).start()
    wn_copy.start()
    cot_copy.start()
    zero_tile = jnp.zeros((BLOCK, BLOCK), BF16)
    tbuf_even[SLOTS] = zero_tile
    tbuf_odd[SLOTS] = zero_tile

    def build(r, slot):
        tbuf = tile_bufs[slot]

        @pl.when(r + 1 < BLOCKS)
        def _():
            tile_copy(r + 1, 1 - slot).start()

        tile_copy(r, slot).wait()
        rows = pl.ds(pl.multiple_of(r * BLOCK, BLOCK), BLOCK)

        def add(k, acc):
            return acc + tbuf[k].astype(F32)

        deg = lax.fori_loop(0, SLOTS, add, jnp.zeros((BLOCK, BLOCK), F32))
        deg = jnp.sum(deg, axis=1, keepdims=True)
        rinv[rows, :] = jnp.broadcast_to(1.0 / deg, (BLOCK, BLOCK))

        def place(s):
            for j in range(BLOCKS):
                k = inv_ref[r, s * BLOCKS + j]
                adj[s, rows, j * BLOCK:(j + 1) * BLOCK] = tbuf[k]

        loop(5, place)

    def product(s, c, first):
        def body(m):
            rows = pl.ds(pl.multiple_of(m * 256, 256), 256)
            part = jnp.dot(adj[s, rows, :], src[s, c], preferred_element_type=F32)
            if first:
                total[c, rows, :] = part
            else:
                total[c, rows, :] += part
        loop(4, body)

    def transpose_into(dst, c, rows, value):
        dst[pl.ds(pl.multiple_of(c * COLS, COLS), COLS), rows] = value.T

    def pre_self(c):
        feat_copy(c).wait()

        def body(i):
            q = i // 2
            rows = pl.ds(pl.multiple_of((i % 2) * 512, 512), 512)
            part = jnp.dot(
                src[0, c, rows, :],
                ws[pl.ds(pl.multiple_of(c * COLS, COLS), COLS),
                   pl.ds(pl.multiple_of(q * COLS, COLS), COLS)],
                preferred_element_type=F32)

            @pl.when(c == 0)
            def _():
                pre[q, rows, :] = part

            @pl.when(c > 0)
            def _():
                pre[q, rows, :] += part
        loop(8, body)

    def flip_features(c):
        def body(m):
            rows = pl.ds(pl.multiple_of(m * 256, 256), 256)
            transpose_into(feat_t, c, rows, src[0, c, rows, :])
        loop(4, body)

    def average(c):
        def scale(m):
            rows = pl.ds(pl.multiple_of(m * BLOCK, BLOCK), BLOCK)
            r = rinv[rows, :]
            value = (total[c, rows, :] * jnp.concatenate([r, r], axis=1)).astype(BF16)
            mean[rows, :] = value
            transpose_into(mean_t, c, rows, value)
        loop(BLOCKS, scale)

        def body(i):
            q = i // 2
            rows = pl.ds(pl.multiple_of((i % 2) * 512, 512), 512)
            pre[q, rows, :] += jnp.dot(
                mean[rows, :],
                wn[pl.ds(pl.multiple_of(c * COLS, COLS), COLS),
                   pl.ds(pl.multiple_of(q * COLS, COLS), COLS)],
                preferred_element_type=F32)
        loop(8, body)

    def tick(t):
        @pl.when(t < PIECES)
        def _():
            f1(t).wait_recv()
            f2(t).start()

        @pl.when(t + AHEAD < PIECES)
        def _():
            f1(t + AHEAD).start()

        @pl.when((t >= 2) & (t < PIECES + 2))
        def _():
            f2(t - 2).wait_recv()
            f3(t - 2).start()

        @pl.when((t >= 4) & (t < PIECES + 4))
        def _():
            f3(t - 4).wait_recv()

        phase = t // 8
        i = t % 8

        @pl.when(t == 0)
        def _():
            ws_copy.wait()

        @pl.when(t < 4)
        def _():
            build(2 * t, 0)
            build(2 * t + 1, 1)
            pre_self(t)

        @pl.when((t >= 4) & (t < 8))
        def _():
            flip_features(t - 4)

        @pl.when(i == 6)
        def _():
            product(0, phase, True)

        @pl.when(i == 7)
        def _():
            fc(phase).wait_recv()
            product(1, phase, False)

        @pl.when((t >= 8) & (i < 5) & (i % 2 == 0))
        def _():
            product(2 + i // 2, phase - 1, False)

        @pl.when(t == 8)
        def _():
            wn_copy.wait()

        @pl.when((t >= 8) & (i == 5))
        def _():
            average(phase - 1)

    loop(PIECES + 6, tick)

    cot_copy.wait()
    c0 = 0.7978845608028654
    c1 = 0.044715

    def hid_copy(q):
        return pltpu.make_async_copy(
            hid.at[q], hidden_ref.at[:, pl.ds(pl.multiple_of(q * COLS, COLS), COLS)],
            hid_sem.at[q])

    def gelu(q):
        cols = pl.ds(pl.multiple_of(q * COLS, COLS), COLS)

        def body(m):
            rows = pl.ds(pl.multiple_of(m * 64, 64), 64)
            v = pre[q, rows, :]
            v2 = v * v
            th = jnp.tanh(c0 * (v + c1 * (v2 * v)))
            half = 0.5 * (1.0 + th)
            hid[q, rows, :] = (v * half).astype(BF16)
            slope = half + (0.5 * v) * (1.0 - th * th) * (c0 + (3.0 * c0 * c1) * v2)
            dpre[rows, :] = (cot[rows, cols].astype(F32) * slope).astype(BF16)
        loop(16, body)
        hid_copy(q).start()

    def keep_rows(u, first, count):
        return (u // 2, pl.ds(pl.multiple_of((u % 2) * 512 + first, 8), count))

    def core_copy(u):
        return pltpu.make_async_remote_copy(
            src_ref=core_out.at[u], dst_ref=core_in.at[u],
            send_sem=core_send.at[u], recv_sem=core_recv.at[u],
            device_id=core_peer, device_id_type=MESH)

    def gradient(q, kind):
        u = 2 * q + kind
        left = feat_t if kind == 0 else mean_t

        def body(lo):
            other = pl.ds(pl.multiple_of(lo * 512 + (1 - core) * 256, 256), 256)
            core_out[u, lo] = jnp.dot(
                left[other, :], dpre[...], preferred_element_type=F32).astype(BF16)
        loop(2, body)
        core_copy(u).start()

        def body2(lo):
            mine = pl.ds(pl.multiple_of(lo * 512 + core * 256, 256), 256)
            qq, rows = keep_rows(u, lo * 256, 256)
            total[qq, rows, :] = jnp.dot(left[mine, :], dpre[...], preferred_element_type=F32)
        loop(2, body2)

    def s1(u, kind, d):
        return pltpu.make_async_remote_copy(
            src_ref=s1_out.at[u, d - 1], dst_ref=s1_in.at[u, d - 1],
            send_sem=s1_send.at[u, d - 1], recv_sem=s1_recv.at[u, d - 1],
            device_id=(x_peer if kind == 0 else y_peer)(d), device_id_type=MESH)

    def s2(u, kind, d):
        return pltpu.make_async_remote_copy(
            src_ref=s2_out.at[u, d - 1], dst_ref=s2_in.at[u, d - 1],
            send_sem=s2_send.at[u, d - 1], recv_sem=s2_recv.at[u, d - 1],
            device_id=(y_peer if kind == 0 else x_peer)(d), device_id_type=MESH)

    def s3(u, d):
        lo, hi = z_ring(d)
        return pltpu.make_async_remote_copy(
            src_ref=acc2.at[u, lo, pl.ds(pl.multiple_of(hi * 8, 8), 8)],
            dst_ref=s3_in.at[u, d - 1],
            send_sem=s3_send.at[u, d - 1], recv_sem=s3_recv.at[u, d - 1],
            device_id=z_dev(d), device_id_type=MESH)

    def half_rows(u, kind, lo, pos):
        if kind == 0:
            first = lo * 256 + pos * 64
            qq, rows = keep_rows(u, first, 64)
            inner = pl.ds(pl.multiple_of(pos * 64, 64), 64)
            return total[qq, rows, :] + core_in[u, lo, inner, :].astype(F32)
        parts = []
        for xx in range(4):
            first = lo * 256 + xx * 64 + pos * 16
            qq, rows = keep_rows(u, first, 16)
            inner = pl.ds(pl.multiple_of(xx * 64 + pos * 16, 16), 16)
            parts.append(total[qq, rows, :] + core_in[u, lo, inner, :].astype(F32))
        return jnp.concatenate(parts, axis=0)

    def stage1(q, kind):
        u = 2 * q + kind
        me = x if kind == 0 else y
        core_copy(u).wait_recv()
        for d in (1, 2, 3):
            for lo in range(2):
                s1_out[u, d - 1, lo] = half_rows(u, kind, lo, (me + d) % 4).astype(BF16)
            s1(u, kind, d).start()
        for lo in range(2):
            acc1[u, lo] = half_rows(u, kind, lo, me)

    def stage2(q, kind):
        u = 2 * q + kind
        me = y if kind == 0 else x
        for d in (1, 2, 3):
            s1(u, kind, d).wait_recv()
        for lo in range(2):
            acc = acc1[u, lo]
            for d in (1, 2, 3):
                acc = acc + s1_in[u, d - 1, lo].astype(F32)
            acc1[u, lo] = acc
        for d in (1, 2, 3):
            pos = (me + d) % 4
            for lo in range(2):
                s2_out[u, d - 1, lo] = acc1[
                    u, lo, pl.ds(pl.multiple_of(pos * 16, 16), 16), :].astype(BF16)
            s2(u, kind, d).start()

    def stage3(q, kind):
        u = 2 * q + kind
        me = y if kind == 0 else x
        for d in (1, 2, 3):
            s2(u, kind, d).wait_recv()
        for lo in range(2):
            acc = acc1[u, lo, pl.ds(pl.multiple_of(me * 16, 16), 16), :]
            for d in (1, 2, 3):
                acc = acc + s2_in[u, d - 1, lo].astype(F32)
            acc2[u, lo] = acc
        for d in (1, 2, 3):
            s3(u, d).start()

    def stage4(q, kind):
        u = 2 * q + kind
        out = gs_ref if kind == 0 else gn_ref
        for d in (1, 2, 3):
            s3(u, d).wait_recv()
        acc = acc2[u, z_lo, pl.ds(pl.multiple_of(z_hi * 8, 8), 8), :]
        for d in (1, 2, 3):
            acc = acc + s3_in[u, d - 1]
        out[:, pl.ds(pl.multiple_of(q * COLS, COLS), COLS)] = acc

    def tail(q):
        @pl.when(q < CHUNKS)
        def _():
            gelu(q)
            gradient(q, 0)

        @pl.when(q > 0)
        def _():
            stage1(q - 1, 1)

        @pl.when(q < CHUNKS)
        def _():
            gradient(q, 1)
            stage1(q, 0)

    loop(CHUNKS + 1, tail)

    def each(f):
        def body(q):
            f(q, 0)
            f(q, 1)
        loop(CHUNKS, body)

    each(stage2)
    each(stage3)
    each(stage4)

    for i in range(3):
        pltpu.make_async_copy(src.at[i + 2], src.at[i + 2], f_send.at[i]).wait()

    def done(q):
        fc(q).wait_send()
        hid_copy(q).wait()
        for kind in range(2):
            u = 2 * q + kind
            core_copy(u).wait_send()
            for d in (1, 2, 3):
                s1(u, kind, d).wait_send()
                s2(u, kind, d).wait_send()
                s3(u, d).wait_send()
    loop(CHUNKS, done)


def fused(inv, features, tiles, w_self, w_neigh, cotangent):
    any_space = pl.BlockSpec(memory_space=pl.ANY)
    vmem = pl.BlockSpec(memory_space=pltpu.VMEM)
    dma = pltpu.SemaphoreType.DMA
    scratch = [
        pltpu.VMEM((5, CHUNKS, ROWS, COLS), BF16),
        pltpu.VMEM((5, ROWS, ROWS), BF16),
        pltpu.VMEM((SLOTS + 1, BLOCK, BLOCK), BF16),
        pltpu.VMEM((SLOTS + 1, BLOCK, BLOCK), BF16),
        pltpu.VMEM((DIM, DIM), BF16),
        pltpu.VMEM((DIM, DIM), BF16),
        pltpu.VMEM((ROWS, DIM), BF16),
        pltpu.VMEM((CHUNKS, ROWS, COLS), F32),
        pltpu.VMEM((CHUNKS, ROWS, COLS), F32),
        pltpu.VMEM((DIM, ROWS), BF16),
        pltpu.VMEM((DIM, ROWS), BF16),
        pltpu.VMEM((ROWS, COLS), BF16),
        pltpu.VMEM((ROWS, BLOCK), F32),
        pltpu.VMEM((ROWS, COLS), BF16),
        pltpu.VMEM((CHUNKS, ROWS, COLS), BF16),
        pltpu.VMEM((UNITS, 2, 256, COLS), BF16),
        pltpu.VMEM((UNITS, 2, 256, COLS), BF16),
        pltpu.VMEM((UNITS, 3, 2, 64, COLS), BF16),
        pltpu.VMEM((UNITS, 3, 2, 64, COLS), BF16),
        pltpu.VMEM((UNITS, 2, 64, COLS), F32),
        pltpu.VMEM((UNITS, 3, 2, 16, COLS), BF16),
        pltpu.VMEM((UNITS, 3, 2, 16, COLS), BF16),
        pltpu.VMEM((UNITS, 2, 16, COLS), F32),
        pltpu.VMEM((UNITS, 3, 8, COLS), F32),
        dma((7,)), dma((2,)), dma((CHUNKS,)), dma((CHUNKS,)), dma((CHUNKS,)),
        dma((3,)), dma((PIECES,)), dma((PIECES,)), dma((PIECES,)),
        dma((UNITS,)), dma((UNITS,)),
        dma((UNITS, 3)), dma((UNITS, 3)), dma((UNITS, 3)), dma((UNITS, 3)),
        dma((UNITS, 3)), dma((UNITS, 3)),
    ]
    return pl.pallas_call(
        kernel,
        out_shape=(
            jax.ShapeDtypeStruct((ROWS, DIM), BF16),
            jax.ShapeDtypeStruct((8, DIM), F32),
            jax.ShapeDtypeStruct((8, DIM), F32),
        ),
        in_specs=[pl.BlockSpec(memory_space=pltpu.SMEM)] + [any_space] * 5,
        out_specs=(any_space, vmem, vmem),
        scratch_shapes=scratch,
        compiler_params=pltpu.CompilerParams(
            collective_id=0, has_side_effects=True, vmem_limit_bytes=62 * 1024 * 1024),
        cost_estimate=pl.CostEstimate(
            flops=20_000_000_000, bytes_accessed=20_000_000, transcendentals=1_000_000),
    )(inv, features, tiles, w_self, w_neigh, cotangent)


def slot_of(slots):
    b = lax.axis_index("blk")
    g = lax.axis_index("grp")
    flip = g + 1 - 2 * (g % 2)
    other = (g - 1 + 2 * (g % 2)) % N_GRP
    devices = jnp.stack([
        b * N_GRP + g, (b + 1 - 2 * (b % 2)) * N_GRP + g, (3 - b) * N_GRP + g,
        b * N_GRP + flip, b * N_GRP + other])
    wanted = (devices[:, None] * BLOCKS + jnp.arange(BLOCKS)[None, :]).reshape(-1)
    match = slots[:, None, :] == wanted[None, :, None]
    place = jnp.arange(SLOTS, dtype=jnp.int32)[None, None, :]
    return jnp.min(jnp.where(match, place, SLOTS), axis=2).astype(jnp.int32)


def on_device(features, tiles, slots, w_self, w_neigh, cotangent):
    return fused(slot_of(slots), features, tiles, w_self, w_neigh, cotangent)


def solution(mesh):
    in_specs = (
        P(("blk", "grp"), None),
        P(("blk", "grp"), None, None, None),
        P(("blk", "grp"), None),
        P(),
        P(),
        P(("blk", "grp"), None),
    )
    out_specs = (P(("blk", "grp"), None), P(("blk", "grp"), None), P(("blk", "grp"), None))
    return jax.shard_map(
        on_device, mesh=mesh, in_specs=in_specs, out_specs=out_specs, check_vma=False
    )
```

time: 1780 us -> 135 us (0.08)
  waiting for transfers between devices: 1430 us -> 0 us
  local copies, waits for them, and re-layouts: 165 us -> 4.49 us
  matrix products: 154 us -> 0 us
  Pallas kernels: 0 us -> 128 us
    unnamed x3 -> x0, waiting for transfers between devices: 662 us -> none
    reduce_scatter x1 -> x0, waiting for transfers between devices: 653 us -> none  [on_device(): lax.psum_scatter(term_neigh, ('blk', 'grp'), scatter_dimension=0, tiled=T...]
    dot_general x28 -> x0, matrix products: 154 us -> none  [the longest x24 133 us: add_slot(): jnp.einsum('rab,rbf->raf', tiles[:, slot], chosen, preferred_element_type...]
    gather x24 -> x0, local copies, waits for them, and re-layouts: 144 us -> none  [add_slot(): chosen = sources[source_id[:, slot], inner[:, slot]]]
    pallas_call x0 -> x1, Pallas kernels: none -> 128 us  [fused(): pl.pallas_call(kernel, out_shape=(jax.ShapeDtypeStruct((ROWS, DIM), BF16)...]
    ppermute x4 -> x0, waiting for transfers between devices: 114 us -> none  [passed_along(): lax.ppermute(array, axis, [(i, (i + by) % peers) for i in range(peers)])]
  transfers between devices with their start and end apart: 6 -> 0, of which waited for: 5 -> 0; matrix products, arithmetic and copies ran while one was open for 2% -> 0% of each run, Pallas kernels for 0% -> 0%
where the time goes in v1:
time: 135 us
  Pallas kernels  128 us (95%)
  local copies, waits for them, and re-layouts  4.49 us (3%)
  other arithmetic  1.47 us (1%)
    pallas_call x1, Pallas kernels, fused(): pl.pallas_call(kernel, out_shape=(jax.ShapeDtypeStruct((ROWS, DIM), BF16)...  128 us
    unnamed x7, local copies, waits for them, and re-layouts  4.33 us

profile of v1, /device:TPU:0, one launch (start us, length us, event | category | flops | bytes accessed | tf_op | source)
XLA Modules:
  0.0 135.1 jit_solution(15998250575196570326)
XLA Ops:
  0.7 0.1 stack.23
  0.8 0.1 iota_add_fusion
  0.8 0.1 add.70
  0.9 1.4 %select_reduce_fusion.inv_ref = s32[8,40]{1,0:T(8,128)} fusion(s32[40]{0:T(128)S(1)} %add.70, s32[8,24]{1,0:T(8,128)} %param.8), kind=kLoop, calls=%fused_computation | loop fusion | flops 22720 | bytes 2208 | tf_op jit(solution)/shard_map/reduce_min | solution.py:523
  2.3 128.4 %shard_map.85 = (bf16[1024,1024]{1,0:T(8,128)(2,1)}, f32[8,1024]{1,0:T(8,128)}, f32[8,1024]{1,0:T(8,128)}) custom-call(s32[8,40]{1,0:T(8,128)} %select_reduce_fusion.inv_ref, bf16[1024,1024]{1,0:T(8,128)(2,1)} %feat_ref.1, bf16[8,24,128,128]{3,2,1,0:T(8,128)(2,1)} %tiles_ref.1, bf16[1024,1024]{1,0:T(8,128)(2,1)} %ws_ref.1, bf16[1024,1024]{1,0:T(8,128)(2,1)} %wn_ref.1, ...), custom_call_target="tpu_custom_call" | custom-call | flops 20000000000 | bytes 20000000 | tf_op jit(solution)/shard_map/pallas_call | solution.py:495
  130.8 0.0 copy-start.1
  130.8 0.0 copy-start
  130.8 3.1 %copy.12 = bf16[1024,1024]{1,0:T(8,128)(2,1)} copy(bf16[1024,1024]{1,0:T(8,128)(2,1)} %get-tuple-element.6) | data formatting | bytes 4194304
  133.9 0.0 copy-done.1
  133.9 0.6 copy.13
  134.5 0.0 copy-done
  134.5 0.6 copy.14
  (1 shorter events, 0.0 us)
Async XLA Ops:
  130.8 3.1 %copy-start.1 = (f32[8,1024]{1,0:T(8,128)S(1)}, f32[8,1024]{1,0:T(8,128)}, u32[]{:S(2)}) copy-start(f32[8,1024]{1,0:T(8,128)} %get-tuple-element.7) | copy-start | bytes 98308
  130.8 3.7 %copy-start = (f32[8,1024]{1,0:T(8,128)S(1)}, f32[8,1024]{1,0:T(8,128)}, u32[]{:S(2)}) copy-start(f32[8,1024]{1,0:T(8,128)} %get-tuple-element.8) | copy-start | bytes 98308

commit v2 on v1

--- a/solution.py
+++ b/solution.py
@@ -17,7 +17,8 @@
 BLOCKS = ROWS // BLOCK
 N_GRP = 32
 PIECES = CHUNKS * BLOCKS
-AHEAD = 4
+AHEAD = 8
+LAG = 3
 UNITS = 2 * CHUNKS
 F32 = jnp.float32
 BF16 = jnp.bfloat16
@@ -30,7 +31,7 @@
 def kernel(
     inv_ref, feat_ref, tiles_ref, ws_ref, wn_ref, cot_ref,
     hidden_ref, gs_ref, gn_ref,
-    src, adj, tbuf_even, tbuf_odd, ws, wn, cot, pre, total, feat_t, mean_t, mean, rinv, dpre, hid,
+    src, adj, tbuf_even, tbuf_odd, ws, wn, cot, pre, total, feat_t, mean_t, mean, rinv, dpre_even, dpre_odd, hid,
     core_out, core_in, s1_out, s1_in, acc1, s2_out, s2_in, acc2, s3_in,
     local_sem, tile_sem, hid_sem, fc_sem, fc_recv, f_send, f1_recv, f2_recv, f3_recv,
     core_send, core_recv, s1_send, s1_recv, s2_send, s2_recv, s3_send, s3_recv,
@@ -148,9 +149,11 @@
         rows = pl.ds(pl.multiple_of(r * BLOCK, BLOCK), BLOCK)
 
         def add(k, acc):
-            return acc + tbuf[k].astype(F32)
-
-        deg = lax.fori_loop(0, SLOTS, add, jnp.zeros((BLOCK, BLOCK), F32))
+            for n in range(4):
+                acc = acc + tbuf[4 * k + n].astype(F32)
+            return acc
+
+        deg = lax.fori_loop(0, SLOTS // 4, add, jnp.zeros((BLOCK, BLOCK), F32))
         deg = jnp.sum(deg, axis=1, keepdims=True)
         rinv[rows, :] = jnp.broadcast_to(1.0 / deg, (BLOCK, BLOCK))
 
@@ -162,63 +165,46 @@
         loop(5, place)
 
     def product(s, c, first):
-        def body(m):
-            rows = pl.ds(pl.multiple_of(m * 256, 256), 256)
-            part = jnp.dot(adj[s, rows, :], src[s, c], preferred_element_type=F32)
-            if first:
-                total[c, rows, :] = part
-            else:
-                total[c, rows, :] += part
-        loop(4, body)
-
-    def transpose_into(dst, c, rows, value):
-        dst[pl.ds(pl.multiple_of(c * COLS, COLS), COLS), rows] = value.T
+        part = jnp.dot(adj[s], src[s, c], preferred_element_type=F32)
+        if first:
+            total[c] = part
+        else:
+            total[c] += part
+
+    def chunk(c):
+        return pl.ds(pl.multiple_of(c * COLS, COLS), COLS)
 
     def pre_self(c):
-        feat_copy(c).wait()
-
-        def body(i):
-            q = i // 2
-            rows = pl.ds(pl.multiple_of((i % 2) * 512, 512), 512)
-            part = jnp.dot(
-                src[0, c, rows, :],
-                ws[pl.ds(pl.multiple_of(c * COLS, COLS), COLS),
-                   pl.ds(pl.multiple_of(q * COLS, COLS), COLS)],
-                preferred_element_type=F32)
+        def body(q):
+            part = jnp.dot(src[0, c], ws[chunk(c), chunk(q)], preferred_element_type=F32)
 
             @pl.when(c == 0)
             def _():
-                pre[q, rows, :] = part
+                pre[q] = part
 
             @pl.when(c > 0)
             def _():
-                pre[q, rows, :] += part
-        loop(8, body)
+                pre[q] += part
+        loop(CHUNKS, body)
+
+    def pre_neigh(c, q):
+        pre[q] += jnp.dot(mean[...], wn[chunk(c), chunk(q)], preferred_element_type=F32)
+
+    def flipped(c):
+        turn = (c + core) % 2
+        return pl.ds(pl.multiple_of(turn * 512 + (c // 2) * 256, 256), 256)
 
     def flip_features(c):
-        def body(m):
-            rows = pl.ds(pl.multiple_of(m * 256, 256), 256)
-            transpose_into(feat_t, c, rows, src[0, c, rows, :])
-        loop(4, body)
+        feat_t[flipped(c), :] = src[0, c].T
 
     def average(c):
         def scale(m):
-            rows = pl.ds(pl.multiple_of(m * BLOCK, BLOCK), BLOCK)
+            rows = pl.ds(pl.multiple_of(m * 256, 256), 256)
             r = rinv[rows, :]
             value = (total[c, rows, :] * jnp.concatenate([r, r], axis=1)).astype(BF16)
             mean[rows, :] = value
-            transpose_into(mean_t, c, rows, value)
-        loop(BLOCKS, scale)
-
-        def body(i):
-            q = i // 2
-            rows = pl.ds(pl.multiple_of((i % 2) * 512, 512), 512)
-            pre[q, rows, :] += jnp.dot(
-                mean[rows, :],
-                wn[pl.ds(pl.multiple_of(c * COLS, COLS), COLS),
-                   pl.ds(pl.multiple_of(q * COLS, COLS), COLS)],
-                preferred_element_type=F32)
-        loop(8, body)
+        loop(4, scale)
+        mean_t[flipped(c), :] = mean[...].T
 
     def tick(t):
         @pl.when(t < PIECES)
@@ -230,58 +216,67 @@
         def _():
             f1(t + AHEAD).start()
 
-        @pl.when((t >= 2) & (t < PIECES + 2))
-        def _():
-            f2(t - 2).wait_recv()
-            f3(t - 2).start()
-
-        @pl.when((t >= 4) & (t < PIECES + 4))
-        def _():
-            f3(t - 4).wait_recv()
+        @pl.when((t >= LAG) & (t < PIECES + LAG))
+        def _():
+            f2(t - LAG).wait_recv()
+            f3(t - LAG).start()
+
+        @pl.when(t >= 2 * LAG)
+        def _():
+            f3(t - 2 * LAG).wait_recv()
 
         phase = t // 8
         i = t % 8
 
-        @pl.when(t == 0)
-        def _():
-            ws_copy.wait()
-
-        @pl.when(t < 4)
-        def _():
-            build(2 * t, 0)
-            build(2 * t + 1, 1)
-            pre_self(t)
-
-        @pl.when((t >= 4) & (t < 8))
-        def _():
-            flip_features(t - 4)
-
-        @pl.when(i == 6)
-        def _():
-            product(0, phase, True)
-
-        @pl.when(i == 7)
-        def _():
-            fc(phase).wait_recv()
-            product(1, phase, False)
-
-        @pl.when((t >= 8) & (i < 5) & (i % 2 == 0))
+        @pl.when((t < 8) & (i % 2 == 0))
+        def _():
+            build(t, 0)
+
+        @pl.when((t < 8) & (i % 2 == 1))
+        def _():
+            build(t, 1)
+
+        @pl.when((t < PIECES) & (((t >= 7) & (i == 1)) | (t == 8)))
+        def _():
+            product(0, phase - (t == 8).astype(jnp.int32), True)
+
+        @pl.when((t < PIECES) & (((t >= 7) & (i == 4)) | (t == 8)))
+        def _():
+            c = phase - (t == 8).astype(jnp.int32)
+            fc(c).wait_recv()
+            product(1, c, False)
+
+        @pl.when((t >= 8) & ((i == 0) | (i == 3) | (i == 5)))
         def _():
             product(2 + i // 2, phase - 1, False)
 
-        @pl.when(t == 8)
-        def _():
-            wn_copy.wait()
-
-        @pl.when((t >= 8) & (i == 5))
+        @pl.when((t == 10) | (t == 15) | (t == 18) | (t == 23))
+        def _():
+            c = (t - 10) // 4
+
+            @pl.when(c == 0)
+            def _():
+                ws_copy.wait()
+                wn_copy.wait()
+
+            pre_self(c)
+            flip_features(c)
+
+        @pl.when((t >= 8) & (t < PIECES) & (i == 6))
         def _():
             average(phase - 1)
-
-    loop(PIECES + 6, tick)
-
+            loop(CHUNKS, lambda q: pre_neigh(phase - 1, q))
+
+    for c in range(CHUNKS):
+        feat_copy(c).wait()
+    loop(PIECES + 2 * LAG, tick)
+    average(CHUNKS - 1)
     cot_copy.wait()
+
     c0 = 0.7978845608028654
     c1 = 0.044715
+
+    dpre = (dpre_even, dpre_odd)
 
     def hid_copy(q):
         return pltpu.make_async_copy(
@@ -289,19 +284,17 @@
             hid_sem.at[q])
 
     def gelu(q):
-        cols = pl.ds(pl.multiple_of(q * COLS, COLS), COLS)
-
-        def body(m):
-            rows = pl.ds(pl.multiple_of(m * 64, 64), 64)
+        dp = dpre[q % 2]
+        for m in range(16):
+            rows = slice(m * 64, m * 64 + 64)
             v = pre[q, rows, :]
             v2 = v * v
             th = jnp.tanh(c0 * (v + c1 * (v2 * v)))
             half = 0.5 * (1.0 + th)
             hid[q, rows, :] = (v * half).astype(BF16)
             slope = half + (0.5 * v) * (1.0 - th * th) * (c0 + (3.0 * c0 * c1) * v2)
-            dpre[rows, :] = (cot[rows, cols].astype(F32) * slope).astype(BF16)
-        loop(16, body)
-        hid_copy(q).start()
+            given = cot[rows, q * COLS:(q + 1) * COLS].astype(F32)
+            dp[rows, :] = (given * slope).astype(BF16)
 
     def keep_rows(u, first, count):
         return (u // 2, pl.ds(pl.multiple_of((u % 2) * 512 + first, 8), count))
@@ -315,19 +308,9 @@
     def gradient(q, kind):
         u = 2 * q + kind
         left = feat_t if kind == 0 else mean_t
-
-        def body(lo):
-            other = pl.ds(pl.multiple_of(lo * 512 + (1 - core) * 256, 256), 256)
-            core_out[u, lo] = jnp.dot(
-                left[other, :], dpre[...], preferred_element_type=F32).astype(BF16)
-        loop(2, body)
-        core_copy(u).start()
-
-        def body2(lo):
-            mine = pl.ds(pl.multiple_of(lo * 512 + core * 256, 256), 256)
-            qq, rows = keep_rows(u, lo * 256, 256)
-            total[qq, rows, :] = jnp.dot(left[mine, :], dpre[...], preferred_element_type=F32)
-        loop(2, body2)
+        grad = jnp.dot(left[...], dpre[q % 2][...], preferred_element_type=F32)
+        total[u // 2, (u % 2) * 512:(u % 2) * 512 + 512, :] = grad[:512]
+        core_out[u] = grad[512:].reshape(2, 256, COLS).astype(BF16)
 
     def s1(u, kind, d):
         return pltpu.make_async_remote_copy(
@@ -414,22 +397,22 @@
             acc = acc + s3_in[u, d - 1]
         out[:, pl.ds(pl.multiple_of(q * COLS, COLS), COLS)] = acc
 
-    def tail(q):
-        @pl.when(q < CHUNKS)
-        def _():
-            gelu(q)
-            gradient(q, 0)
-
-        @pl.when(q > 0)
-        def _():
+    pre_neigh(CHUNKS - 1, 0)
+    gelu(0)
+    for q in range(CHUNKS):
+        if q + 1 < CHUNKS:
+            pre_neigh(CHUNKS - 1, q + 1)
+            gelu(q + 1)
+        gradient(q, 0)
+        gradient(q, 1)
+        hid_copy(q).start()
+        core_copy(2 * q).start()
+        core_copy(2 * q + 1).start()
+        if q > 0:
+            stage1(q - 1, 0)
             stage1(q - 1, 1)
-
-        @pl.when(q < CHUNKS)
-        def _():
-            gradient(q, 1)
-            stage1(q, 0)
-
-    loop(CHUNKS + 1, tail)
+    stage1(CHUNKS - 1, 0)
+    stage1(CHUNKS - 1, 1)
 
     def each(f):
         def body(q):
@@ -475,6 +458,7 @@
         pltpu.VMEM((DIM, ROWS), BF16),
         pltpu.VMEM((ROWS, COLS), BF16),
         pltpu.VMEM((ROWS, BLOCK), F32),
+        pltpu.VMEM((ROWS, COLS), BF16),
         pltpu.VMEM((ROWS, COLS), BF16),
         pltpu.VMEM((CHUNKS, ROWS, COLS), BF16),
         pltpu.VMEM((UNITS, 2, 256, COLS), BF16),

time: 135 us -> 104 us (0.77)
  Pallas kernels: 128 us -> 97.6 us
    pallas_call x1, Pallas kernels: 128 us -> 97.6 us  [fused(): pl.pallas_call(kernel, out_shape=(jax.ShapeDtypeStruct((ROWS, DIM), BF16)...]
where the time goes in v2:
time: 104 us
  Pallas kernels  97.6 us (94%)
  local copies, waits for them, and re-layouts  4.49 us (4%)
  other arithmetic  1.47 us (1%)
    pallas_call x1, Pallas kernels, fused(): pl.pallas_call(kernel, out_shape=(jax.ShapeDtypeStruct((ROWS, DIM), BF16)...  97.6 us
    unnamed x7, local copies, waits for them, and re-layouts  4.33 us

profile of v2, /device:TPU:0, one launch (start us, length us, event | category | flops | bytes accessed | tf_op | source)
XLA Modules:
  0.0 104.3 jit_solution(1564792889666680923)
XLA Ops:
  0.7 0.1 stack.23
  0.8 0.1 iota_add_fusion
  0.8 0.1 add.70
  0.9 1.4 %select_reduce_fusion.inv_ref = s32[8,40]{1,0:T(8,128)} fusion(s32[40]{0:T(128)S(1)} %add.70, s32[8,24]{1,0:T(8,128)} %param.8), kind=kLoop, calls=%fused_computation | loop fusion | flops 22720 | bytes 2208 | tf_op jit(solution)/shard_map/reduce_min | solution.py:507
  2.3 97.6 %shard_map.85 = (bf16[1024,1024]{1,0:T(8,128)(2,1)}, f32[8,1024]{1,0:T(8,128)}, f32[8,1024]{1,0:T(8,128)}) custom-call(s32[8,40]{1,0:T(8,128)} %select_reduce_fusion.inv_ref, bf16[1024,1024]{1,0:T(8,128)(2,1)} %feat_ref.1, bf16[8,24,128,128]{3,2,1,0:T(8,128)(2,1)} %tiles_ref.1, bf16[1024,1024]{1,0:T(8,128)(2,1)} %ws_ref.1, bf16[1024,1024]{1,0:T(8,128)(2,1)} %wn_ref.1, ...), custom_call_target="tpu_custom_call" | custom-call | flops 20000000000 | bytes 20000000 | tf_op jit(solution)/shard_map/pallas_call | solution.py:479
  99.9 0.0 copy-start.1
  99.9 0.0 copy-start
  99.9 3.1 %copy.12 = bf16[1024,1024]{1,0:T(8,128)(2,1)} copy(bf16[1024,1024]{1,0:T(8,128)(2,1)} %get-tuple-element.6) | data formatting | bytes 4194304
  103.0 0.0 copy-done.1
  103.0 0.6 copy.13
  103.6 0.0 copy-done
  103.6 0.6 copy.14
  (1 shorter events, 0.0 us)
Async XLA Ops:
  99.9 3.1 %copy-start.1 = (f32[8,1024]{1,0:T(8,128)S(1)}, f32[8,1024]{1,0:T(8,128)}, u32[]{:S(2)}) copy-start(f32[8,1024]{1,0:T(8,128)} %get-tuple-element.7) | copy-start | bytes 98308
  99.9 3.7 %copy-start = (f32[8,1024]{1,0:T(8,128)S(1)}, f32[8,1024]{1,0:T(8,128)}, u32[]{:S(2)}) copy-start(f32[8,1024]{1,0:T(8,128)} %get-tuple-element.8) | copy-start | bytes 98308

commit v3 on v2

v3 whole, which is shorter than its diff:
```python
import functools

import jax
import jax.numpy as jnp
from jax import lax
from jax.experimental import pallas as pl
from jax.experimental.pallas import tpu as pltpu
from jax.sharding import PartitionSpec as P

MESH = pl.DeviceIdType.MESH
BLOCK = 128
SLOTS = 24
ROWS = 1024
DIM = 1024
COLS = 256
CHUNKS = DIM // COLS
BLOCKS = ROWS // BLOCK
N_GRP = 32
PIECES = CHUNKS * BLOCKS
AHEAD = 8
LAG = 3
UNITS = 2 * CHUNKS
F32 = jnp.float32
BF16 = jnp.bfloat16


def loop(count, body):
    lax.fori_loop(0, count, lambda i, _: (body(i), None)[1], None)


def kernel(
    slots_ref, feat_ref, tiles_ref, ws_ref, wn_ref, cot_ref,
    hidden_ref, gs_ref, gn_ref,
    src, adj, tbuf_even, tbuf_odd, ws, wn, cot, pre, total, left_self, left_neigh, mean, mean_in,
    rinv, table, inv_ref, dcat, hid, s1_out, s1_in, acc1, s2_out, s2_in, acc2, s3_in,
    local_sem, tile_sem, hid_sem, fc_sem, fc_recv, f_send, f1_recv, f2_recv, f3_recv,
    m_send, m_recv, dp_send, dp_recv, rs_send, s1_recv, s2_recv, s3_recv,
):
    b = lax.axis_index("blk")
    g = lax.axis_index("grp")
    z_lo = b // 2
    core = b % 2
    z_hi = g % 2
    y = (g // 2) % 4
    x = g // 8

    def at(bb, gg):
        return (bb, gg)

    core_peer = at(z_lo * 2 + (1 - core), g)
    z_peer = at(3 - b, g)
    hi_peer = at(3 - b, z_hi * (g - 1) + (1 - z_hi) * (g + 1))
    step = 2 - 4 * z_hi
    out_peer = at(b, (g + step + N_GRP) % N_GRP)
    in_peer = at(b, (g - step + N_GRP) % N_GRP)

    def x_peer(d):
        return at(b, ((x + d) % 4) * 8 + y * 2 + z_hi)

    def y_peer(d):
        return at(b, x * 8 + ((y + d) % 4) * 2 + z_hi)

    def z_ring(d):
        lo = (z_lo + d % 2) % 2
        hi = (z_hi + d // 2) % 2
        return lo, hi

    def z_dev(d):
        lo, hi = z_ring(d)
        return at(lo * 2 + core, x * 8 + y * 2 + hi)

    peers = [core_peer, z_peer, hi_peer, out_peer, in_peer]
    for d in (1, 2, 3):
        peers += [x_peer(d), y_peer(d), z_dev(d)]

    def feat_copy(c):
        return pltpu.make_async_copy(
            feat_ref.at[:, pl.ds(c * COLS, COLS)], src.at[0, c], local_sem.at[c])

    tile_bufs = (tbuf_even, tbuf_odd)

    def tile_copy(r, slot):
        return pltpu.make_async_copy(
            tiles_ref.at[r], tile_bufs[slot].at[pl.ds(0, SLOTS)], tile_sem.at[slot])

    ws_copy = pltpu.make_async_copy(ws_ref, ws, local_sem.at[4])
    wn_copy = pltpu.make_async_copy(wn_ref, wn, local_sem.at[5])
    cot_copy = pltpu.make_async_copy(cot_ref, cot, local_sem.at[6])

    barrier = pltpu.get_barrier_semaphore()
    for p in peers:
        pl.semaphore_signal(barrier, inc=1, device_id=p, device_id_type=MESH)
    tile_copy(0, 0).start()
    for c in range(CHUNKS):
        feat_copy(c).start()
    pl.semaphore_wait(barrier, len(peers))

    def piece(p):
        return p // BLOCKS, pl.ds(pl.multiple_of((p % BLOCKS) * BLOCK, BLOCK), BLOCK)

    def f1(p):
        c, rows = piece(p)
        return pltpu.make_async_remote_copy(
            src_ref=feat_ref.at[rows, pl.ds(pl.multiple_of(c * COLS, COLS), COLS)],
            dst_ref=src.at[2, c, rows],
            send_sem=f_send.at[0], recv_sem=f1_recv.at[p],
            device_id=z_peer, device_id_type=MESH)

    def f2(p):
        c, rows = piece(p)
        return pltpu.make_async_remote_copy(
            src_ref=src.at[2, c, rows], dst_ref=src.at[3, c, rows],
            send_sem=f_send.at[1], recv_sem=f2_recv.at[p],
            device_id=hi_peer, device_id_type=MESH)

    def f3(p):
        c, rows = piece(p)
        return pltpu.make_async_remote_copy(
            src_ref=src.at[3, c, rows], dst_ref=src.at[4, c, rows],
            send_sem=f_send.at[2], recv_sem=f3_recv.at[p],
            device_id=out_peer, device_id_type=MESH)

    def fc(c):
        return pltpu.make_async_remote_copy(
            src_ref=feat_ref.at[:, pl.ds(pl.multiple_of(c * COLS, COLS), COLS)],
            dst_ref=src.at[1, c],
            send_sem=fc_sem.at[c], recv_sem=fc_recv.at[c],
            device_id=core_peer, device_id_type=MESH)

    for p in range(AHEAD):
        f1(p).start()
    fc(0).start()
    ws_copy.start()
    zero_tile = jnp.zeros((BLOCK, BLOCK), BF16)
    tbuf_even[SLOTS] = zero_tile
    tbuf_odd[SLOTS] = zero_tile

    def find_slots():
        here = b * N_GRP + g
        devices = (here, here + (1 - 2 * core) * N_GRP, (3 - b) * N_GRP + g,
                   here + 1 - 2 * z_hi, b * N_GRP + (g - 1 + 2 * z_hi + N_GRP) % N_GRP)
        named = slots_ref[...]
        owner = named // BLOCKS
        column = jnp.full(named.shape, BLOCK, jnp.int32)
        for s, device in enumerate(devices):
            column = jnp.where(owner == device, s * BLOCKS + named % BLOCKS, column)
        lane = lax.broadcasted_iota(jnp.int32, (BLOCKS, BLOCK), 1)
        found = jnp.full((BLOCKS, BLOCK), SLOTS, jnp.int32)
        for k in reversed(range(SLOTS)):
            found = jnp.where(column[:, k:k + 1] == lane, k, found)
        table[...] = found
        copy = pltpu.make_async_copy(table, inv_ref, local_sem.at[7])
        copy.start()
        copy.wait()

    def build(r, slot):
        tbuf = tile_bufs[slot]

        @pl.when(r + 1 < BLOCKS)
        def _():
            tile_copy(r + 1, 1 - slot).start()

        tile_copy(r, slot).wait()
        rows = pl.ds(pl.multiple_of(r * BLOCK, BLOCK), BLOCK)

        def add(k, acc):
            for n in range(4):
                acc = acc + tbuf[4 * k + n].astype(F32)
            return acc

        deg = lax.fori_loop(0, SLOTS // 4, add, jnp.zeros((BLOCK, BLOCK), F32))
        deg = jnp.sum(deg, axis=1, keepdims=True)
        rinv[rows, :] = jnp.broadcast_to(1.0 / deg, (BLOCK, BLOCK))

        def place(s):
            for j in range(BLOCKS):
                k = inv_ref[r, s * BLOCKS + j]
                adj[s, rows, j * BLOCK:(j + 1) * BLOCK] = tbuf[k]

        loop(5, place)

    def product(s, c, first):
        part = jnp.dot(adj[s], src[s, c], preferred_element_type=F32)
        if first:
            total[c] = part
        else:
            total[c] += part

    def chunk(c):
        return pl.ds(pl.multiple_of(c * COLS, COLS), COLS)

    def pre_self(c):
        part = jnp.dot(src[0, c], ws[chunk(c), :], preferred_element_type=F32)
        for q in range(CHUNKS):
            @pl.when(c == 0)
            def _():
                pre[q] = part[:, q * COLS:(q + 1) * COLS]

            @pl.when(c > 0)
            def _():
                pre[q] += part[:, q * COLS:(q + 1) * COLS]

    def pre_neigh(c):
        part = jnp.dot(mean[c], wn[chunk(c), :], preferred_element_type=F32)
        for q in range(CHUNKS):
            pre[q] += part[:, q * COLS:(q + 1) * COLS]

    def half(lo):
        return slice(lo * COLS, (lo + 1) * COLS)

    def flip_self(lo):
        left_self[half(lo), :ROWS] = src[0, 2 * lo + core].T

    def flip_self_partner(lo):
        left_self[half(lo), ROWS:] = src[1, 2 * lo + core].T

    def flip_neigh(lo):
        left_neigh[half(lo), :ROWS] = mean[2 * lo + core].T

    def mean_copy(lo):
        return pltpu.make_async_remote_copy(
            src_ref=mean.at[2 * lo + 1 - core], dst_ref=mean_in.at[lo],
            send_sem=m_send.at[lo], recv_sem=m_recv.at[lo],
            device_id=core_peer, device_id_type=MESH)

    def flip_neigh_partner(lo):
        mean_copy(lo).wait_recv()
        left_neigh[half(lo), ROWS:] = mean_in[lo].T

    def average(c):
        def scale(m):
            rows = pl.ds(pl.multiple_of(m * 256, 256), 256)
            r = rinv[rows, :]
            value = (total[c, rows, :] * jnp.concatenate([r, r], axis=1)).astype(BF16)
            mean[c, rows, :] = value
        loop(4, scale)

        @pl.when(c % 2 != core)
        def _():
            mean_copy(c // 2).start()

    def tick(t):
        @pl.when(t < PIECES)
        def _():
            f1(t).wait_recv()
            f2(t).start()

        @pl.when(t + AHEAD < PIECES)
        def _():
            f1(t + AHEAD).start()

        @pl.when((t >= LAG) & (t < PIECES + LAG))
        def _():
            f2(t - LAG).wait_recv()
            f3(t - LAG).start()

        @pl.when(t >= 2 * LAG)
        def _():
            f3(t - 2 * LAG).wait_recv()

        phase = t // 8
        i = t % 8

        @pl.when((t < 6) & (t % 2 == 0))
        def _():
            build(t + 2, 0)

        @pl.when((t < 6) & (t % 2 == 1))
        def _():
            build(t + 2, 1)

        @pl.when((t == 6) | ((t >= 8) & (t < PIECES) & (i == 1)))
        def _():
            product(0, phase, True)

        @pl.when((t == 7) | ((t >= 8) & (t < PIECES) & (i == 4)))
        def _():
            fc(phase).wait_recv()
            product(1, phase, False)

        @pl.when((t >= 8) & ((i == 0) | (i == 3) | (i == 5)))
        def _():
            product(2 + i // 2, phase - 1, False)

        @pl.when((t >= 4) & (t < PIECES - 8) & (i == 4))
        def _():
            fc(phase + 1).start()

        @pl.when(t == 6)
        def _():
            wn_copy.start()

        @pl.when(t == 10)
        def _():
            ws_copy.wait()

        @pl.when(((t >= 8) & (t < PIECES) & (i == 2)) | (t == 36))
        def _():
            pre_self(phase - 1)

        @pl.when(t == 10)
        def _():
            flip_self(0)

        @pl.when(t == 18)
        def _():
            flip_self(1)
            flip_self_partner(0)

        @pl.when(t == 20)
        def _():
            cot_copy.start()

        @pl.when(t == 33)
        def _():
            flip_self_partner(1)

        @pl.when(t == 34)
        def _():
            flip_neigh(0)
            flip_neigh_partner(0)

        @pl.when((t >= 8) & (t < PIECES) & (i == 6))
        def _():
            average(phase - 1)

        @pl.when((t >= 8) & (t < PIECES) & (i == 7))
        def _():
            @pl.when(t == 15)
            def _():
                wn_copy.wait()

            pre_neigh(phase - 1)

    for c in range(CHUNKS):
        feat_copy(c).wait()
    find_slots()
    build(0, 0)
    build(1, 1)
    loop(PIECES + 2 * LAG, tick)
    average(CHUNKS - 1)
    cot_copy.wait()

    c0 = 0.7978845608028654
    c1 = 0.044715

    def hid_copy(q):
        return pltpu.make_async_copy(
            hid.at[q], hidden_ref.at[:, pl.ds(pl.multiple_of(q * COLS, COLS), COLS)],
            hid_sem.at[q])

    def dp_copy(q):
        return pltpu.make_async_remote_copy(
            src_ref=dcat.at[q, pl.ds(0, ROWS)], dst_ref=dcat.at[q, pl.ds(ROWS, ROWS)],
            send_sem=dp_send.at[q], recv_sem=dp_recv.at[q],
            device_id=core_peer, device_id_type=MESH)

    def gelu(q):
        pre[q] += jnp.dot(
            mean[CHUNKS - 1], wn[DIM - COLS:, q * COLS:(q + 1) * COLS], preferred_element_type=F32)
        for m in range(16):
            rows = slice(m * 64, m * 64 + 64)
            v = pre[q, rows, :]
            v2 = v * v
            th = jnp.tanh(c0 * (v + c1 * (v2 * v)))
            upper = 0.5 * (1.0 + th)
            hid[q, rows, :] = (v * upper).astype(BF16)
            slope = upper + (0.5 * v) * (1.0 - th * th) * (c0 + (3.0 * c0 * c1) * v2)
            given = cot[rows, q * COLS:(q + 1) * COLS].astype(F32)
            dcat[q, rows, :] = (given * slope).astype(BF16)
        dp_copy(q).start()
        hid_copy(q).start()

    FIRST = "xyzxyzxy"

    def peer(axis, d):
        return {"x": x_peer, "y": y_peer, "z": z_dev}[axis](d)

    def kept(u, first, count):
        return total[u // 2, pl.ds(pl.multiple_of((u % 2) * 512 + first, 8), count), :]

    def share(u, d):
        axis = FIRST[u]
        if axis == "x":
            pos = (x + d) % 4
            return jnp.concatenate([kept(u, lo * 256 + pos * 64, 64) for lo in range(2)], axis=0)
        if axis == "y":
            pos = (y + d) % 4
            return jnp.concatenate(
                [kept(u, lo * 256 + xx * 64 + pos * 16, 16) for lo in range(2) for xx in range(4)],
                axis=0)
        lo, hi = z_ring(d)
        return jnp.concatenate(
            [kept(u, lo * 256 + k * 16 + hi * 8, 8) for k in range(16)], axis=0)

    def s1(u, d):
        return pltpu.make_async_remote_copy(
            src_ref=s1_out.at[u, d - 1], dst_ref=s1_in.at[u, d - 1],
            send_sem=rs_send.at[0], recv_sem=s1_recv.at[u, d - 1],
            device_id=peer(FIRST[u], d), device_id_type=MESH)

    def second(u):
        return {"x": "y", "y": "x", "z": "x"}[FIRST[u]]

    def third(u):
        return {"x": "z", "y": "z", "z": "y"}[FIRST[u]]

    def place(axis, d):
        if axis == "z":
            lo, hi = z_ring(d)
            return lo * 2 + hi
        return ((x if axis == "x" else y) + d) % 4

    def s2(u, d):
        return pltpu.make_async_remote_copy(
            src_ref=s2_out.at[u, d - 1], dst_ref=s2_in.at[u, d - 1],
            send_sem=rs_send.at[1], recv_sem=s2_recv.at[u, d - 1],
            device_id=peer(second(u), d), device_id_type=MESH)

    def s3(u, d):
        return pltpu.make_async_remote_copy(
            src_ref=acc2.at[u, pl.ds(pl.multiple_of(place(third(u), d) * 8, 8), 8)],
            dst_ref=s3_in.at[u, d - 1],
            send_sem=rs_send.at[2], recv_sem=s3_recv.at[u, d - 1],
            device_id=peer(third(u), d), device_id_type=MESH)

    def gradient(q, kind):
        left = left_self if kind == 0 else left_neigh
        total[q, kind * 512:kind * 512 + 512, :] = jnp.dot(
            left[...], dcat[q], preferred_element_type=F32)

    def stage1(u):
        for d in (1, 2, 3):
            s1_out[u, d - 1] = share(u, d).astype(BF16)
            s1(u, d).start()

    def part2(u, d):
        pos = place(second(u), d)
        if FIRST[u] == "z":
            return acc1[u, pl.ds(pl.multiple_of(pos * 32, 32), 32), :]
        return jnp.concatenate(
            [acc1[u, pl.ds(pl.multiple_of(lo * 64 + pos * 16, 16), 16), :] for lo in range(2)], axis=0)

    def stage2(u):
        acc = share(u, 0)
        for d in (1, 2, 3):
            s1(u, d).wait_recv()
            acc = acc + s1_in[u, d - 1].astype(F32)
        acc1[u] = acc
        for d in (1, 2, 3):
            s2_out[u, d - 1] = part2(u, d).astype(BF16)
            s2(u, d).start()

    def stage3(u):
        acc = part2(u, 0)
        for d in (1, 2, 3):
            s2(u, d).wait_recv()
            acc = acc + s2_in[u, d - 1].astype(F32)
        acc2[u] = acc
        for d in (1, 2, 3):
            s3(u, d).start()

    def stage4(u):
        out = gs_ref if u % 2 == 0 else gn_ref
        acc = acc2[u, pl.ds(pl.multiple_of(place(third(u), 0) * 8, 8), 8), :]
        for d in (1, 2, 3):
            s3(u, d).wait_recv()
            acc = acc + s3_in[u, d - 1]
        out[:, (u // 2) * COLS:(u // 2 + 1) * COLS] = acc

    gelu(0)
    gelu(1)
    flip_neigh(1)
    for q in range(CHUNKS):
        if 0 < q < CHUNKS - 1:
            gelu(q + 1)
        dp_copy(q).wait_recv()
        gradient(q, 0)
        stage1(2 * q)
        if q == 0:
            flip_neigh_partner(1)
        gradient(q, 1)
        stage1(2 * q + 1)
        if q == 2:
            stage2(0)
            stage2(1)
    for u in (2, 3, 4):
        stage2(u)
    stage3(0)
    stage3(1)
    stage2(5)
    stage3(2)
    stage3(3)
    stage2(6)
    stage2(7)
    for u in (4, 5, 6, 7):
        stage3(u)
    for u in range(UNITS):
        stage4(u)

    for i in range(3):
        pltpu.make_async_copy(src.at[i + 2], src.at[i + 2], f_send.at[i]).wait()
    for i, whole in enumerate((s1_out, s2_out, s3_in)):
        pltpu.make_async_copy(whole, whole, rs_send.at[i]).wait()
    for lo in range(2):
        mean_copy(lo).wait_send()
    for q in range(CHUNKS):
        fc(q).wait_send()
        dp_copy(q).wait_send()
        hid_copy(q).wait()


def fused(slots, features, tiles, w_self, w_neigh, cotangent):
    any_space = pl.BlockSpec(memory_space=pl.ANY)
    vmem = pl.BlockSpec(memory_space=pltpu.VMEM)
    dma = pltpu.SemaphoreType.DMA
    scratch = [
        pltpu.VMEM((5, CHUNKS, ROWS, COLS), BF16),
        pltpu.VMEM((5, ROWS, ROWS), BF16),
        pltpu.VMEM((SLOTS + 1, BLOCK, BLOCK), BF16),
        pltpu.VMEM((SLOTS + 1, BLOCK, BLOCK), BF16),
        pltpu.VMEM((DIM, DIM), BF16),
        pltpu.VMEM((DIM, DIM), BF16),
        pltpu.VMEM((ROWS, DIM), BF16),
        pltpu.VMEM((CHUNKS, ROWS, COLS), F32),
        pltpu.VMEM((CHUNKS, ROWS, COLS), F32),
        pltpu.VMEM((DIM // 2, 2 * ROWS), BF16),
        pltpu.VMEM((DIM // 2, 2 * ROWS), BF16),
        pltpu.VMEM((CHUNKS, ROWS, COLS), BF16),
        pltpu.VMEM((2, ROWS, COLS), BF16),
        pltpu.VMEM((ROWS, BLOCK), F32),
        pltpu.VMEM((BLOCKS, BLOCK), jnp.int32),
        pltpu.SMEM((BLOCKS, BLOCK), jnp.int32),
        pltpu.VMEM((CHUNKS, 2 * ROWS, COLS), BF16),
        pltpu.VMEM((CHUNKS, ROWS, COLS), BF16),
        pltpu.VMEM((UNITS, 3, 128, COLS), BF16),
        pltpu.VMEM((UNITS, 3, 128, COLS), BF16),
        pltpu.VMEM((UNITS, 128, COLS), F32),
        pltpu.VMEM((UNITS, 3, 32, COLS), BF16),
        pltpu.VMEM((UNITS, 3, 32, COLS), BF16),
        pltpu.VMEM((UNITS, 32, COLS), F32),
        pltpu.VMEM((UNITS, 3, 8, COLS), F32),
        dma((8,)), dma((2,)), dma((CHUNKS,)), dma((CHUNKS,)), dma((CHUNKS,)),
        dma((3,)), dma((PIECES,)), dma((PIECES,)), dma((PIECES,)),
        dma((2,)), dma((2,)), dma((CHUNKS,)), dma((CHUNKS,)), dma((3,)),
        dma((UNITS, 3)), dma((UNITS, 3)), dma((UNITS, 3)),
    ]
    return pl.pallas_call(
        kernel,
        out_shape=(
            jax.ShapeDtypeStruct((ROWS, DIM), BF16),
            jax.ShapeDtypeStruct((8, DIM), F32),
            jax.ShapeDtypeStruct((8, DIM), F32),
        ),
        in_specs=[vmem] + [any_space] * 5,
        out_specs=(any_space, vmem, vmem),
        scratch_shapes=scratch,
        compiler_params=pltpu.CompilerParams(
            collective_id=0, has_side_effects=True, vmem_limit_bytes=62 * 1024 * 1024),
        cost_estimate=pl.CostEstimate(
            flops=20_000_000_000, bytes_accessed=20_000_000, transcendentals=1_000_000),
    )(slots, features, tiles, w_self, w_neigh, cotangent)


def settle_kernel(hid_ref, gs_ref, gn_ref, hid_out, gs_out, gn_out, buf, gbuf, sem):
    ways = [(hid_ref.at[pl.ds(i * BLOCK, BLOCK)], buf.at[pl.ds(i * BLOCK, BLOCK)],
             hid_out.at[pl.ds(i * BLOCK, BLOCK)]) for i in range(BLOCKS)]
    ways += [(gs_ref, gbuf.at[0], gs_out), (gn_ref, gbuf.at[1], gn_out)]
    first = [pltpu.make_async_copy(a, m, sem.at[0, i]) for i, (a, m, _) in enumerate(ways)]
    last = [pltpu.make_async_copy(m, c, sem.at[1, i]) for i, (_, m, c) in enumerate(ways)]
    for copy in first:
        copy.start()
    for one, two in zip(first, last):
        one.wait()
        two.start()
    for copy in last:
        copy.wait()


def settled(hidden, grad_self, grad_neigh):
    outs = (hidden, grad_self, grad_neigh)
    return pl.pallas_call(
        settle_kernel,
        out_shape=tuple(jax.ShapeDtypeStruct(a.shape, a.dtype) for a in outs),
        in_specs=[pl.BlockSpec(memory_space=pl.ANY)] * 3,
        out_specs=(pl.BlockSpec(memory_space=pl.ANY),) * 3,
        scratch_shapes=[
            pltpu.VMEM((ROWS, DIM), BF16), pltpu.VMEM((2, 8, DIM), F32),
            pltpu.SemaphoreType.DMA((2, BLOCKS + 2))],
        compiler_params=pltpu.CompilerParams(vmem_limit_bytes=62 * 1024 * 1024),
        cost_estimate=pl.CostEstimate(flops=0, bytes_accessed=4_300_000, transcendentals=0),
    )(*outs)


def on_device(features, tiles, slots, w_self, w_neigh, cotangent):
    return settled(*fused(slots, features, tiles, w_self, w_neigh, cotangent))


def solution(mesh):
    in_specs = (
        P(("blk", "grp"), None),
        P(("blk", "grp"), None, None, None),
        P(("blk", "grp"), None),
        P(),
        P(),
        P(("blk", "grp"), None),
    )
    out_specs = (P(("blk", "grp"), None), P(("blk", "grp"), None), P(("blk", "grp"), None))
    return jax.shard_map(
        on_device, mesh=mesh, in_specs=in_specs, out_specs=out_specs, check_vma=False
    )
```

time: 104 us -> 101 us (0.971)
  local copies, waits for them, and re-layouts: 4.49 us -> 0 us
  Pallas kernels: 97.6 us -> 99.7 us
  other arithmetic: 1.47 us -> 0 us
    unnamed x7 -> x0, local copies, waits for them, and re-layouts: 4.33 us -> none
    pallas_call x0 -> x1, Pallas kernels: none -> 2.44 us  [settled(): pl.pallas_call(settle_kernel, out_shape=tuple((jax.ShapeDtypeStruct(a.sha...]
    reduce_min x1 -> x0, other arithmetic: 1.39 us -> none  [slot_of(): return jnp.min(jnp.where(match, place, SLOTS), axis=2).astype(jnp.int32)]
where the time goes in v3:
time: 101 us
  Pallas kernels  99.7 us (99%)
    pallas_call x1, Pallas kernels, fused(): pl.pallas_call(kernel, out_shape=(jax.ShapeDtypeStruct((ROWS, DIM), BF16)...  97.3 us
    pallas_call x1, Pallas kernels, settled(): pl.pallas_call(settle_kernel, out_shape=tuple((jax.ShapeDtypeStruct(a.sha...  2.44 us

profile of v3, /device:TPU:0, one launch (start us, length us, event | category | flops | bytes accessed | tf_op | source)
XLA Modules:
  0.0 100.5 jit_solution(4170632500485869459)
XLA Ops:
  0.6 97.3 %shard_map.85 = (bf16[1024,1024]{1,0:T(8,128)(2,1)}, f32[8,1024]{1,0:T(8,128)}, f32[8,1024]{1,0:T(8,128)}) custom-call(s32[8,24]{1,0:T(8,128)} %slots_ref.1, bf16[1024,1024]{1,0:T(8,128)(2,1)} %feat_ref.1, bf16[8,24,128,128]{3,2,1,0:T(8,128)(2,1)} %tiles_ref.1, bf16[1024,1024]{1,0:T(8,128)(2,1)} %ws_ref.1, bf16[1024,1024]{1,0:T(8,128)(2,1)} %wn_ref.1, ...), custom_call_target="tpu_custom_call" | custom-call | flops 20000000000 | bytes 20000000 | tf_op jit(solution)/shard_map/pallas_call | solution.py:548
  97.9 2.4 %shard_map.86 = (bf16[1024,1024]{1,0:T(8,128)(2,1)}, f32[8,1024]{1,0:T(8,128)}, f32[8,1024]{1,0:T(8,128)}) custom-call(bf16[1024,1024]{1,0:T(8,128)(2,1)} %get-tuple-element.6.hid_ref, f32[8,1024]{1,0:T(8,128)} %get-tuple-element.7.gs_ref, f32[8,1024]{1,0:T(8,128)} %get-tuple-element.8.gn_ref), custom_call_target="tpu_custom_call" | custom-call | bytes 4300000 | tf_op jit(solution)/shard_map/pallas_call | solution.py:582

commit v4 on v3

--- a/solution.py
+++ b/solution.py
@@ -91,6 +91,7 @@
     for p in peers:
         pl.semaphore_signal(barrier, inc=1, device_id=p, device_id_type=MESH)
     tile_copy(0, 0).start()
+    tile_copy(1, 1).start()
     for c in range(CHUNKS):
         feat_copy(c).start()
     pl.semaphore_wait(barrier, len(peers))
@@ -156,10 +157,6 @@
     def build(r, slot):
         tbuf = tile_bufs[slot]
 
-        @pl.when(r + 1 < BLOCKS)
-        def _():
-            tile_copy(r + 1, 1 - slot).start()
-
         tile_copy(r, slot).wait()
         rows = pl.ds(pl.multiple_of(r * BLOCK, BLOCK), BLOCK)
 
@@ -178,6 +175,10 @@
                 adj[s, rows, j * BLOCK:(j + 1) * BLOCK] = tbuf[k]
 
         loop(5, place)
+
+        @pl.when(r + 2 < BLOCKS)
+        def _():
+            tile_copy(r + 2, slot).start()
 
     def product(s, c, first):
         part = jnp.dot(adj[s], src[s, c], preferred_element_type=F32)
@@ -192,6 +193,11 @@
     def pre_self(c):
         part = jnp.dot(src[0, c], ws[chunk(c), :], preferred_element_type=F32)
         for q in range(CHUNKS):
+            pre[q] += part[:, q * COLS:(q + 1) * COLS]
+
+    def pre_neigh(c):
+        part = jnp.dot(mean[c], wn[chunk(c), :], preferred_element_type=F32)
+        for q in range(CHUNKS):
             @pl.when(c == 0)
             def _():
                 pre[q] = part[:, q * COLS:(q + 1) * COLS]
@@ -199,11 +205,6 @@
             @pl.when(c > 0)
             def _():
                 pre[q] += part[:, q * COLS:(q + 1) * COLS]
-
-    def pre_neigh(c):
-        part = jnp.dot(mean[c], wn[chunk(c), :], preferred_element_type=F32)
-        for q in range(CHUNKS):
-            pre[q] += part[:, q * COLS:(q + 1) * COLS]
 
     def half(lo):
         return slice(lo * COLS, (lo + 1) * COLS)
@@ -261,27 +262,34 @@
         phase = t // 8
         i = t % 8
 
-        @pl.when((t < 6) & (t % 2 == 0))
-        def _():
-            build(t + 2, 0)
-
-        @pl.when((t < 6) & (t % 2 == 1))
-        def _():
-            build(t + 2, 1)
-
-        @pl.when((t == 6) | ((t >= 8) & (t < PIECES) & (i == 1)))
-        def _():
-            product(0, phase, True)
-
-        @pl.when((t == 7) | ((t >= 8) & (t < PIECES) & (i == 4)))
-        def _():
-            fc(phase).wait_recv()
-            product(1, phase, False)
-
-        @pl.when((t >= 8) & ((i == 0) | (i == 3) | (i == 5)))
+        @pl.when((t < 8) & (t % 2 == 0))
+        def _():
+            build(t, 0)
+
+        @pl.when((t < 8) & (t % 2 == 1))
+        def _():
+            build(t, 1)
+
+        @pl.when((t == 8) | ((t >= 8) & (t < PIECES) & (i == 1)))
+        def _():
+            product(0, phase - (t == 8).astype(jnp.int32), True)
+
+        @pl.when((t == 10) | ((t >= 8) & (t < PIECES) & (i == 4)))
+        def _():
+            c = phase - (t == 10).astype(jnp.int32)
+            fc(c).wait_recv()
+            product(1, c, False)
+
+        @pl.when((t >= 8) & (t < PIECES + 5) & ((i == 0) | (i == 3) | (i == 5)))
         def _():
             product(2 + i // 2, phase - 1, False)
 
+        @pl.when((t == PIECES + 2) | (t == PIECES + 5))
+        def _():
+            rows = pl.ds(pl.multiple_of((t - PIECES - 2) // 3 * 512, 512), 512)
+            total[CHUNKS - 1] += jnp.dot(
+                adj[4, :, rows], src[4, CHUNKS - 1, rows, :], preferred_element_type=F32)
+
         @pl.when((t >= 4) & (t < PIECES - 8) & (i == 4))
         def _():
             fc(phase + 1).start()
@@ -290,21 +298,24 @@
         def _():
             wn_copy.start()
 
-        @pl.when(t == 10)
+        @pl.when(t == 12)
         def _():
             ws_copy.wait()
 
-        @pl.when(((t >= 8) & (t < PIECES) & (i == 2)) | (t == 36))
-        def _():
-            pre_self(phase - 1)
-
-        @pl.when(t == 10)
+        @pl.when((t == 18) | (t == 26) | (t == 34) | (t == 36))
+        def _():
+            pre_self(phase - 2 + t // 36)
+
+        @pl.when(t == 14)
         def _():
             flip_self(0)
 
-        @pl.when(t == 18)
+        @pl.when(t == 22)
         def _():
             flip_self(1)
+
+        @pl.when(t == 30)
+        def _():
             flip_self_partner(0)
 
         @pl.when(t == 20)
@@ -335,8 +346,6 @@
     for c in range(CHUNKS):
         feat_copy(c).wait()
     find_slots()
-    build(0, 0)
-    build(1, 1)
     loop(PIECES + 2 * LAG, tick)
     average(CHUNKS - 1)
     cot_copy.wait()
@@ -361,11 +370,12 @@
         for m in range(16):
             rows = slice(m * 64, m * 64 + 64)
             v = pre[q, rows, :]
-            v2 = v * v
-            th = jnp.tanh(c0 * (v + c1 * (v2 * v)))
-            upper = 0.5 * (1.0 + th)
-            hid[q, rows, :] = (v * upper).astype(BF16)
-            slope = upper + (0.5 * v) * (1.0 - th * th) * (c0 + (3.0 * c0 * c1) * v2)
+            p = (c0 * c1) * (v * v)
+            th = jnp.tanh(v * (c0 + p))
+            upper = 0.5 + 0.5 * th
+            out = v * upper
+            hid[q, rows, :] = out.astype(BF16)
+            slope = upper + out * (1.0 - th) * (c0 + 3.0 * p)
             given = cot[rows, q * COLS:(q + 1) * COLS].astype(F32)
             dcat[q, rows, :] = (given * slope).astype(BF16)
         dp_copy(q).start()
@@ -488,12 +498,9 @@
         stage2(u)
     stage3(0)
     stage3(1)
-    stage2(5)
-    stage3(2)
-    stage3(3)
-    stage2(6)
-    stage2(7)
-    for u in (4, 5, 6, 7):
+    for u in (5, 6, 7):
+        stage2(u)
+    for u in range(2, UNITS):
         stage3(u)
     for u in range(UNITS):
         stage4(u)

time: 101 us -> 99.1 us (0.981)
  Pallas kernels: 99.7 us -> 98.1 us
    pallas_call x1, Pallas kernels: 97.3 us -> 95.7 us  [fused(): pl.pallas_call(kernel, out_shape=(jax.ShapeDtypeStruct((ROWS, DIM), BF16)...]
where the time goes in v4:
time: 99.1 us; the launch traced here: 98.9 us
  Pallas kernels  98.1 us (99%)
    pallas_call x1, Pallas kernels, fused(): pl.pallas_call(kernel, out_shape=(jax.ShapeDtypeStruct((ROWS, DIM), BF16)...  95.7 us
    pallas_call x1, Pallas kernels, settled(): pl.pallas_call(settle_kernel, out_shape=tuple((jax.ShapeDtypeStruct(a.sha...  2.44 us

profile of v4, /device:TPU:0, one launch (start us, length us, event | category | flops | bytes accessed | tf_op | source)
XLA Modules:
  0.0 98.9 jit_solution(983930348193542681)
XLA Ops:
  0.6 95.7 %shard_map.85 = (bf16[1024,1024]{1,0:T(8,128)(2,1)}, f32[8,1024]{1,0:T(8,128)}, f32[8,1024]{1,0:T(8,128)}) custom-call(s32[8,24]{1,0:T(8,128)} %slots_ref.1, bf16[1024,1024]{1,0:T(8,128)(2,1)} %feat_ref.1, bf16[8,24,128,128]{3,2,1,0:T(8,128)(2,1)} %tiles_ref.1, bf16[1024,1024]{1,0:T(8,128)(2,1)} %ws_ref.1, bf16[1024,1024]{1,0:T(8,128)(2,1)} %wn_ref.1, ...), custom_call_target="tpu_custom_call" | custom-call | flops 20000000000 | bytes 20000000 | tf_op jit(solution)/shard_map/pallas_call | solution.py:555
  96.3 2.4 %shard_map.86 = (bf16[1024,1024]{1,0:T(8,128)(2,1)}, f32[8,1024]{1,0:T(8,128)}, f32[8,1024]{1,0:T(8,128)}) custom-call(bf16[1024,1024]{1,0:T(8,128)(2,1)} %get-tuple-element.6.hid_ref, f32[8,1024]{1,0:T(8,128)} %get-tuple-element.7.gs_ref, f32[8,1024]{1,0:T(8,128)} %get-tuple-element.8.gn_ref), custom_call_target="tpu_custom_call" | custom-call | bytes 4300000 | tf_op jit(solution)/shard_map/pallas_call | solution.py:589

commit v5 on v4

--- a/solution.py
+++ b/solution.py
@@ -70,7 +70,7 @@
         return at(lo * 2 + core, x * 8 + y * 2 + hi)
 
     peers = [core_peer, z_peer, hi_peer, out_peer, in_peer]
-    for d in (1, 2, 3):
+    for d in (2, 1, 3):
         peers += [x_peer(d), y_peer(d), z_dev(d)]
 
     def feat_copy(c):
@@ -440,7 +440,7 @@
             left[...], dcat[q], preferred_element_type=F32)
 
     def stage1(u):
-        for d in (1, 2, 3):
+        for d in (2, 1, 3):
             s1_out[u, d - 1] = share(u, d).astype(BF16)
             s1(u, d).start()
 
@@ -453,27 +453,27 @@
 
     def stage2(u):
         acc = share(u, 0)
-        for d in (1, 2, 3):
+        for d in (2, 1, 3):
             s1(u, d).wait_recv()
             acc = acc + s1_in[u, d - 1].astype(F32)
         acc1[u] = acc
-        for d in (1, 2, 3):
+        for d in (2, 1, 3):
             s2_out[u, d - 1] = part2(u, d).astype(BF16)
             s2(u, d).start()
 
     def stage3(u):
         acc = part2(u, 0)
-        for d in (1, 2, 3):
+        for d in (2, 1, 3):
             s2(u, d).wait_recv()
             acc = acc + s2_in[u, d - 1].astype(F32)
         acc2[u] = acc
-        for d in (1, 2, 3):
+        for d in (2, 1, 3):
             s3(u, d).start()
 
     def stage4(u):
         out = gs_ref if u % 2 == 0 else gn_ref
         acc = acc2[u, pl.ds(pl.multiple_of(place(third(u), 0) * 8, 8), 8), :]
-        for d in (1, 2, 3):
+        for d in (2, 1, 3):
             s3(u, d).wait_recv()
             acc = acc + s3_in[u, d - 1]
         out[:, (u // 2) * COLS:(u // 2 + 1) * COLS] = acc

time: 99.1 us -> 97.9 us (0.988)
  Pallas kernels: 98.1 us -> 96.9 us
    pallas_call x1, Pallas kernels: 95.7 us -> 94.5 us  [fused(): pl.pallas_call(kernel, out_shape=(jax.ShapeDtypeStruct((ROWS, DIM), BF16)...]
where the time goes in v5:
time: 97.9 us; the launch traced here: 97.7 us
  Pallas kernels  96.9 us (99%)
    pallas_call x1, Pallas kernels, fused(): pl.pallas_call(kernel, out_shape=(jax.ShapeDtypeStruct((ROWS, DIM), BF16)...  94.5 us
    pallas_call x1, Pallas kernels, settled(): pl.pallas_call(settle_kernel, out_shape=tuple((jax.ShapeDtypeStruct(a.sha...  2.44 us

profile of v5, /device:TPU:0, one launch (start us, length us, event | category | flops | bytes accessed | tf_op | source)
XLA Modules:
  0.0 97.7 jit_solution(1918918354155820684)
XLA Ops:
  0.6 94.5 %shard_map.85 = (bf16[1024,1024]{1,0:T(8,128)(2,1)}, f32[8,1024]{1,0:T(8,128)}, f32[8,1024]{1,0:T(8,128)}) custom-call(s32[8,24]{1,0:T(8,128)} %slots_ref.1, bf16[1024,1024]{1,0:T(8,128)(2,1)} %feat_ref.1, bf16[8,24,128,128]{3,2,1,0:T(8,128)(2,1)} %tiles_ref.1, bf16[1024,1024]{1,0:T(8,128)(2,1)} %ws_ref.1, bf16[1024,1024]{1,0:T(8,128)(2,1)} %wn_ref.1, ...), custom_call_target="tpu_custom_call" | custom-call | flops 20000000000 | bytes 20000000 | tf_op jit(solution)/shard_map/pallas_call | solution.py:555
  95.1 2.4 %shard_map.86 = (bf16[1024,1024]{1,0:T(8,128)(2,1)}, f32[8,1024]{1,0:T(8,128)}, f32[8,1024]{1,0:T(8,128)}) custom-call(bf16[1024,1024]{1,0:T(8,128)(2,1)} %get-tuple-element.6.hid_ref, f32[8,1024]{1,0:T(8,128)} %get-tuple-element.7.gs_ref, f32[8,1024]{1,0:T(8,128)} %get-tuple-element.8.gn_ref), custom_call_target="tpu_custom_call" | custom-call | bytes 4300000 | tf_op jit(solution)/shard_map/pallas_call | solution.py:589

commit v6 on v5

--- a/solution.py
+++ b/solution.py
@@ -17,8 +17,10 @@
 BLOCKS = ROWS // BLOCK
 N_GRP = 32
 PIECES = CHUNKS * BLOCKS
-AHEAD = 8
-LAG = 3
+SENT = 2 * PIECES
+SENT_ROWS = 64
+AHEAD = 32
+LAG = 6
 UNITS = 2 * CHUNKS
 F32 = jnp.float32
 BF16 = jnp.bfloat16
@@ -97,7 +99,8 @@
     pl.semaphore_wait(barrier, len(peers))
 
     def piece(p):
-        return p // BLOCKS, pl.ds(pl.multiple_of((p % BLOCKS) * BLOCK, BLOCK), BLOCK)
+        count = ROWS // SENT_ROWS
+        return p // count, pl.ds(pl.multiple_of((p % count) * SENT_ROWS, SENT_ROWS), SENT_ROWS)
 
     def f1(p):
         c, rows = piece(p)
@@ -241,16 +244,16 @@
             mean_copy(c // 2).start()
 
     def tick(t):
-        @pl.when(t < PIECES)
+        @pl.when(t < SENT)
         def _():
             f1(t).wait_recv()
             f2(t).start()
 
-        @pl.when(t + AHEAD < PIECES)
+        @pl.when(t + AHEAD < SENT)
         def _():
             f1(t + AHEAD).start()
 
-        @pl.when((t >= LAG) & (t < PIECES + LAG))
+        @pl.when((t >= LAG) & (t < SENT + LAG))
         def _():
             f2(t - LAG).wait_recv()
             f3(t - LAG).start()
@@ -259,6 +262,11 @@
         def _():
             f3(t - 2 * LAG).wait_recv()
 
+        @pl.when(t % 2 == 1)
+        def _():
+            jobs(t // 2)
+
+    def jobs(t):
         phase = t // 8
         i = t % 8
 
@@ -346,7 +354,7 @@
     for c in range(CHUNKS):
         feat_copy(c).wait()
     find_slots()
-    loop(PIECES + 2 * LAG, tick)
+    loop(SENT + 2 * LAG, tick)
     average(CHUNKS - 1)
     cot_copy.wait()
 
@@ -410,10 +418,10 @@
             device_id=peer(FIRST[u], d), device_id_type=MESH)
 
     def second(u):
-        return {"x": "y", "y": "x", "z": "x"}[FIRST[u]]
+        return {"x": "z", "y": "z", "z": "x"}[FIRST[u]]
 
     def third(u):
-        return {"x": "z", "y": "z", "z": "y"}[FIRST[u]]
+        return {"x": "y", "y": "x", "z": "y"}[FIRST[u]]
 
     def place(axis, d):
         if axis == "z":
@@ -445,11 +453,13 @@
             s1(u, d).start()
 
     def part2(u, d):
-        pos = place(second(u), d)
         if FIRST[u] == "z":
+            pos = place(second(u), d)
             return acc1[u, pl.ds(pl.multiple_of(pos * 32, 32), 32), :]
+        lo, hi = z_ring(d)
         return jnp.concatenate(
-            [acc1[u, pl.ds(pl.multiple_of(lo * 64 + pos * 16, 16), 16), :] for lo in range(2)], axis=0)
+            [acc1[u, pl.ds(pl.multiple_of(lo * 64 + k * 16 + hi * 8, 8), 8), :] for k in range(4)],
+            axis=0)
 
     def stage2(u):
         acc = share(u, 0)
@@ -548,7 +558,7 @@
         pltpu.VMEM((UNITS, 32, COLS), F32),
         pltpu.VMEM((UNITS, 3, 8, COLS), F32),
         dma((8,)), dma((2,)), dma((CHUNKS,)), dma((CHUNKS,)), dma((CHUNKS,)),
-        dma((3,)), dma((PIECES,)), dma((PIECES,)), dma((PIECES,)),
+        dma((3,)), dma((SENT,)), dma((SENT,)), dma((SENT,)),
         dma((2,)), dma((2,)), dma((CHUNKS,)), dma((CHUNKS,)), dma((3,)),
         dma((UNITS, 3)), dma((UNITS, 3)), dma((UNITS, 3)),
     ]

time: 97.9 us -> 97.7 us (level)
  no operation moved by 1% of the time
where the time goes in v6:
time: 97.7 us; the launch traced here: 97.5 us
  Pallas kernels  96.7 us (99%)
    pallas_call x1, Pallas kernels, fused(): pl.pallas_call(kernel, out_shape=(jax.ShapeDtypeStruct((ROWS, DIM), BF16)...  94.3 us
    pallas_call x1, Pallas kernels, settled(): pl.pallas_call(settle_kernel, out_shape=tuple((jax.ShapeDtypeStruct(a.sha...  2.44 us

profile of v6, /device:TPU:0, one launch (start us, length us, event | category | flops | bytes accessed | tf_op | source)
XLA Modules:
  0.0 97.5 jit_solution(14353181040978776759)
XLA Ops:
  0.6 94.3 %shard_map.85 = (bf16[1024,1024]{1,0:T(8,128)(2,1)}, f32[8,1024]{1,0:T(8,128)}, f32[8,1024]{1,0:T(8,128)}) custom-call(s32[8,24]{1,0:T(8,128)} %slots_ref.1, bf16[1024,1024]{1,0:T(8,128)(2,1)} %feat_ref.1, bf16[8,24,128,128]{3,2,1,0:T(8,128)(2,1)} %tiles_ref.1, bf16[1024,1024]{1,0:T(8,128)(2,1)} %ws_ref.1, bf16[1024,1024]{1,0:T(8,128)(2,1)} %wn_ref.1, ...), custom_call_target="tpu_custom_call" | custom-call | flops 20000000000 | bytes 20000000 | tf_op jit(solution)/shard_map/pallas_call | solution.py:565
  94.9 2.4 %shard_map.86 = (bf16[1024,1024]{1,0:T(8,128)(2,1)}, f32[8,1024]{1,0:T(8,128)}, f32[8,1024]{1,0:T(8,128)}) custom-call(bf16[1024,1024]{1,0:T(8,128)(2,1)} %get-tuple-element.6.hid_ref, f32[8,1024]{1,0:T(8,128)} %get-tuple-element.7.gs_ref, f32[8,1024]{1,0:T(8,128)} %get-tuple-element.8.gn_ref), custom_call_target="tpu_custom_call" | custom-call | bytes 4300000 | tf_op jit(solution)/shard_map/pallas_call | solution.py:599
